TPU v7x, 32 devices: a whole 2x2x4 slice. The times are simulated.
32 devices in a mesh: section: 2 (over core), dp: 16 (over z, y, x).
Axes of the slice: x: 2, y: 2, z: 4, core: 2. Of those that a mesh axis runs over, the one named last changes fastest.
Arguments:
- x_in: bfloat16 [4096, 1024], P('dp'), may hold values from -6 to 6
- cotangent: bfloat16 [4096, 1024], P('dp'), may hold values from -6 to 6
- doc_lengths: int32 [32, 8], P('dp'), may hold values from 1 to 64, 128 in all within a row
- w_qkv: float32 [2, 1024, 3072], P('section', 'dp'), may hold values from -0.1875 to 0.1875
- w_out: float32 [2, 1024, 1024], P('section', 'dp'), may hold values from -0.5 to 0.5
- w_up: float32 [2, 1024, 4096], P('section', 'dp'), may hold values from -0.1875 to 0.1875
- w_down: float32 [2, 4096, 1024], P('section', 'dp'), may hold values from -0.09375 to 0.09375
- vectors: float32 [2, 11264], P('section', 'dp'), may hold values from -1 to 3.5, as said below
- m_qkv: float32 [2, 1024, 3072], P('section', 'dp'), may hold values from -0.00012207031 to 0.00012207031
- m_out: float32 [2, 1024, 1024], P('section', 'dp'), may hold values from -0.00012207031 to 0.00012207031
- m_up: float32 [2, 1024, 4096], P('section', 'dp'), may hold values from -0.00012207031 to 0.00012207031
- m_down: float32 [2, 4096, 1024], P('section', 'dp'), may hold values from -0.00012207031 to 0.00012207031
- m_vectors: float32 [2, 11264], P('section', 'dp'), may hold values from -0.00048828125 to 0.00048828125
- v_qkv: float32 [2, 1024, 3072], P('section', 'dp'), may hold values from 1.0441334e-09 to 1.6714075e-08
- v_out: float32 [2, 1024, 1024], P('section', 'dp'), may hold values from 1.0441334e-09 to 1.6714075e-08
- v_up: float32 [2, 1024, 4096], P('section', 'dp'), may hold values from 1.0441334e-09 to 1.6714075e-08
- v_down: float32 [2, 4096, 1024], P('section', 'dp'), may hold values from 1.0441334e-09 to 1.6714075e-08
- v_vectors: float32 [2, 11264], P('section', 'dp'), may hold values from 1.6674374e-08 to 2.6599596e-07
Outputs:
- hidden_out: bfloat16 [2, 4096, 1024], P('section', 'dp')
- input_grads: bfloat16 [2, 4096, 1024], P('section', 'dp')
- new_qkv: float32 [2, 1024, 3072], P('section', 'dp')
- new_out: float32 [2, 1024, 1024], P('section', 'dp')
- new_up: float32 [2, 1024, 4096], P('section', 'dp')
- new_down: float32 [2, 4096, 1024], P('section', 'dp')
- new_vectors: float32 [2, 11264], P('section', 'dp')
- first_qkv: float32 [2, 1024, 3072], P('section', 'dp')
- first_out: float32 [2, 1024, 1024], P('section', 'dp')
- first_up: float32 [2, 1024, 4096], P('section', 'dp')
- first_down: float32 [2, 4096, 1024], P('section', 'dp')
- first_vectors: float32 [2, 11264], P('section', 'dp')
- second_qkv: float32 [2, 1024, 3072], P('section', 'dp')
- second_out: float32 [2, 1024, 1024], P('section', 'dp')
- second_up: float32 [2, 1024, 4096], P('section', 'dp')
- second_down: float32 [2, 4096, 1024], P('section', 'dp')
- second_vectors: float32 [2, 11264], P('section', 'dp')
- grad_norm: float32 [], replicated
Inputs may be any that keep to these rules, and one draw needn't show every extreme that they name: `doc_lengths`: each row gives, in order, the lengths of the 8 documents of one packed sequence; they sum to 128, and the longest has exactly 64 tokens. `vectors`: per block, in order: query, key and value biases, output bias, up bias, down bias, the norm's gain, the norm's bias.
All inputs are finite; a program needn't handle non-finite values.
Results may differ from a plain program's by a relative error of at most 0.018.
The roundings to bfloat16 on the way count: a program that leaves them out, or rounds other values in their place, can miss the bound.
Values may be sent and summed in bfloat16 or wider, within the bound.
No kernel may reach another device: no remote copies, remote signals or barrier semaphores. Data moves between devices by JAX's collectives and lax.ppermute only.
A program may use at most 512 MiB of HBM per device.

v0:
```python
import functools

import jax
import jax.numpy as jnp
from jax import lax
from jax.experimental import pallas as pl
from jax.experimental.pallas import tpu as pltpu
from jax.sharding import PartitionSpec as P

D = 1024
FF = 4096
HEADS = 16
HEAD_DIM = 64
ROT = 16
STEP = 10


NORM_EPS = 1e-05
BETA_ONE = 0.9
BETA_TWO = 0.95
LEARN_RATE = 0.05
VECTOR_RATE = 0.3
WEIGHT_DECAY = 0.01
CLIP_LEVEL = 1.0
ADAM_EPS = 1e-08

AXES = ("section", "dp")
GROUP = 4
SPREAD = 1
LOW = jnp.bfloat16
F32 = jnp.float32
SIDE = D // GROUP
UNITS = FF // GROUP
MIXED = 3 * SIDE + UNITS
PART = MIXED // 2
WIRE = PART + 128


class Ring:
    def __init__(self, count):
        self.count = count
        self.low = count // (GROUP * SPREAD)
        self.size = SPREAD * self.low
        self.bits = self.size.bit_length() - 1

    def index(self, g, t):
        return ((t // self.low) * GROUP + g) * self.low + t % self.low

    def group_of(self, dp):
        return (dp // self.low) % GROUP

    def spot_of(self, dp):
        return (dp // (GROUP * self.low)) * self.low + dp % self.low

    def order(self, core):
        steps = list(range(self.bits))
        if SPREAD > 1 or core == 1:
            steps.reverse()
        return steps

    def turn(self, slot, core):
        return sum(((slot >> s) & 1) << b for s, b in enumerate(self.order(core)))

    def slot(self, difference, core):
        return sum(((difference >> b) & 1) << s for s, b in enumerate(self.order(core)))


class Place:
    def __init__(self):
        self.ring = Ring(lax.axis_size("dp"))
        self.core = lax.axis_index("section")
        dp = lax.axis_index("dp")
        self.group = self.ring.group_of(dp)
        self.spot = self.ring.spot_of(dp)

    def info(self):
        return jnp.stack([self.core, self.group, self.spot]).astype(jnp.int32)

    def move(self, block, where):
        ring = self.ring
        route = []
        for core in range(2):
            for g in range(GROUP):
                for t in range(ring.size):
                    c, h, u = where(core, g, t)
                    route.append((core * ring.count + ring.index(g, t), c * ring.count + ring.index(h, u)))
        return lax.ppermute(block, AXES, route)

    def sibling(self, block):
        return self.move(block, lambda c, g, t: (1 - c, g, t))

    def member(self, block, distance):
        return self.move(block, lambda c, g, t: (c, g ^ distance, t))

    def toward(self, block, step):
        return self.move(block, lambda c, g, t: (c, g ^ (2, 1)[(step + c) % 2], t))

    def across(self, block, step):
        return self.move(block, lambda c, g, t: (c, g, t ^ (1 << self.ring.order(c)[step])))


def take(block, index, axis=0):
    return lax.dynamic_index_in_dim(block, index, axis, keepdims=False)


def after(block, *waited):
    return lax.optimization_barrier((block, waited))[0]


def dot(left, right):
    return jnp.dot(left, right, preferred_element_type=F32)


def dot_cols(left, right):
    return lax.dot_general(left, right, (((1,), (1,)), ((), ())), preferred_element_type=F32)


def dot_rows(left, right):
    return lax.dot_general(left, right, (((0,), (0,)), ((), ())), preferred_element_type=F32)


def full_spec(shape):
    return pl.BlockSpec(shape, lambda *_: (0,) * len(shape))


def far_spec():
    return pl.BlockSpec(memory_space=pltpu.HBM)


def far(block):
    return pltpu.with_memory_space_constraint(block, pltpu.HBM)


def any_spec():
    return pl.BlockSpec(memory_space=pl.ANY)


def smem_spec():
    return pl.BlockSpec(memory_space=pltpu.SMEM)


def shaped(shape, dtype):
    return jax.ShapeDtypeStruct(shape, dtype)


def kernel_params(mebibytes):
    return pltpu.CompilerParams(vmem_limit_bytes=mebibytes * 1024 * 1024)


def up_pieces():
    run = UNITS // SPREAD
    cuts = sorted({0, PART - 3 * SIDE, UNITS} | {run * i for i in range(SPREAD)})
    pieces = []
    for begin, end in zip(cuts[:-1], cuts[1:]):
        column = 3 * SIDE + begin
        pieces.append((begin, column // PART, column % PART, end - begin))
    return pieces


def up_column(g, local):
    run = UNITS // SPREAD
    return (local // run * GROUP + g) * run + local % run


def qkv_column(kind, run, g):
    width = SIDE // SPREAD
    return ((kind * SPREAD + run) * GROUP + g) * width


def pack_kernel(info, qkv_hbm, out_hbm, up_hbm, down_hbm, vec, keep_qu, send_qu, keep_od, send_od, *scratch):
    w_qkv, w_out, w_up, w_down, sems = scratch
    pairs = ((qkv_hbm, w_qkv), (up_hbm, w_up), (down_hbm, w_down), (out_hbm, w_out))
    copies = [pltpu.make_async_copy(far.at[0], near, sems.at[i]) for i, (far, near) in enumerate(pairs)]
    for copy in copies:
        copy.start()
    rows = w_qkv.shape[0]
    ff_rows = w_down.shape[0]
    width = SIDE // SPREAD
    core = info[0]

    def write_qu(halves):
        for g in range(GROUP):
            for kind in range(3):
                for run in range(SPREAD):
                    at = (kind * SPREAD + run) * width
                    column = qkv_column(kind, run, g)
                    halves[0][g, :, at : at + width] = w_qkv[:, column : column + width].astype(LOW)
            for local, half, at, length in up_pieces():
                column = up_column(g, local)
                halves[half][g, :, at : at + length] = w_up[:, column : column + length].astype(LOW)
            for half in range(2):
                halves[half][g, :, PART:WIRE] = vec[...]

    def write_od(halves):
        for half in range(2):
            columns = slice(half * (D // 2), (half + 1) * (D // 2))
            halves[half][0:ff_rows] = w_down[:, columns].astype(LOW)
            halves[half][ff_rows : ff_rows + rows] = w_out[:, columns].astype(LOW)

    for first, last, write, kept, sent in ((0, 2, write_qu, keep_qu, send_qu), (2, 4, write_od, keep_od, send_od)):
        for copy in copies[first:last]:
            copy.wait()
        pl.when(core == 0)(functools.partial(write, (kept, sent)))
        pl.when(core == 1)(functools.partial(write, (sent, kept)))


def pack(info, w_qkv, w_out, w_up, w_down, vec):
    rows, ff_rows = w_qkv.shape[1], w_down.shape[1]
    qu = shaped((GROUP, rows, WIRE), LOW)
    od = shaped((ff_rows + rows, D // 2), LOW)
    return pl.pallas_call(
        pack_kernel,
        out_shape=(qu, qu, od, od),
        in_specs=[smem_spec()] + [far_spec()] * 4 + [full_spec(vec.shape)],
        out_specs=tuple(full_spec(a.shape) for a in (qu, qu, od, od)),
        scratch_shapes=[pltpu.VMEM(a.shape[1:], F32) for a in (w_qkv, w_out, w_up, w_down)]
        + [pltpu.SemaphoreType.DMA((4,))],
        compiler_params=kernel_params(20),
        name="pack_weights",
    )(info, far(w_qkv), far(w_out), far(w_up), far(w_down), vec)


def stack_kernel(*refs):
    for i, ref in enumerate(refs[:-1]):
        refs[-1][0, i] = ref[...]


def stack_members(pieces):
    out = shaped((1, len(pieces), *pieces[0].shape), LOW)
    return pl.pallas_call(
        stack_kernel,
        out_shape=out,
        in_specs=[full_spec(a.shape) for a in pieces],
        out_specs=full_spec(out.shape),
        compiler_params=kernel_params(16),
        cost_estimate=cost(50 * 10**9, 1024 * 1024),
        name="stack_members",
    )(*pieces)


def weight_copies(ring, info, parts, wqu, wout, wdown, sems):
    core, group, spot = info[0], info[1], info[2]
    qu_copies, od_copies = [], []
    count = len(parts) // 4
    for which in range(2):
        half = core if which == 0 else 1 - core
        qu_at = pl.multiple_of(half * PART, 128)
        od_at = pl.multiple_of(half * (D // 2), 128)
        slot = 0
        for piece in range(count):
            qu, od = parts[2 * count * which + piece], parts[2 * count * which + count + piece]
            rows = qu.shape[2]
            ff_rows = od.shape[1] - rows
            for i in range(qu.shape[0]):
                straight, turned = ring.turn(slot, 0), ring.turn(slot, 1)
                there = spot ^ (straight + half * (turned - straight))
                slot += 1
                ff_row = pl.multiple_of(there * ff_rows, ff_rows)
                out_row = pl.multiple_of(there * rows, rows)
                far = wdown.at[pl.ds(ff_row, ff_rows), pl.ds(od_at, D // 2)]
                od_copies.append(pltpu.make_async_copy(od.at[i, pl.ds(0, ff_rows)], far, sems.at[0]))
                far = wout.at[pl.ds(out_row, rows), pl.ds(od_at, D // 2)]
                od_copies.append(pltpu.make_async_copy(od.at[i, pl.ds(ff_rows, rows)], far, sems.at[0]))
                for r in range(GROUP):
                    row = pl.multiple_of(ring.index(group ^ r, there) * rows, rows)
                    far = wqu.at[pl.ds(row, rows), pl.ds(qu_at, PART)]
                    qu_copies.append(pltpu.make_async_copy(qu.at[i, r, :, pl.ds(0, PART)], far, sems.at[1]))
    return qu_copies, od_copies


def head_masks(dtype):
    lane = lax.broadcasted_iota(jnp.int32, (1, SIDE), 1) // HEAD_DIM
    return [(lane == h).astype(dtype) for h in range(SIDE // HEAD_DIM)]


def by_head(parts):
    lane = lax.broadcasted_iota(jnp.int32, (1, SIDE), 1) // HEAD_DIM
    total = parts[-1]
    for h in range(len(parts) - 2, -1, -1):
        total = jnp.where(lane == h, parts[h], total)
    return total


def turning(cosine, sine, back):
    lane = lax.broadcasted_iota(jnp.int32, sine.shape, 1) % HEAD_DIM
    first = jnp.where(lane < ROT // 2, sine, 0.0)
    second = jnp.where(lane < ROT // 2, 0.0, sine)
    if back:
        second = -second
    else:
        first = -first
    wide = SIDE // cosine.shape[1]
    return [jnp.concatenate([a] * wide, axis=1) for a in (cosine, first, second)]


def turn(part, tables):
    cosine, first, second = tables
    ahead = pltpu.roll(part, SIDE - ROT // 2, 1)
    behind = pltpu.roll(part, ROT // 2, 1)
    return part * cosine + ahead * first + behind * second


def normalise(rows):
    centered = rows - jnp.mean(rows, axis=-1, keepdims=True)
    variance = jnp.mean(centered * centered, axis=-1, keepdims=True)
    return centered * lax.rsqrt(variance + NORM_EPS)


def no_wait():
    pass


def forward_part(x_refs, tables, vecs, wqu, wout, wdown, kept, z_refs, waits, done, normed_ref=None):
    cosine, sine, mask = tables
    b_qkv, b_up, gain, ln_bias = vecs
    y, qkv, probs, mixed, active, slope = kept
    rows = z_refs[0].shape[0]
    for r in range(GROUP):
        normed = normalise(x_refs[r][0:rows, :].astype(F32))
        if normed_ref is not None:
            normed_ref[r * rows : (r + 1) * rows, :] = normed
        y[r * rows : (r + 1) * rows, :] = (normed * gain[...] + ln_bias[...]).astype(LOW)
    done(0)
    waits[0]()
    waits[2]()
    forth = turning(cosine[...], sine[...], False)
    for kind in range(3):
        columns = slice(kind * SIDE, (kind + 1) * SIDE)
        part = dot(y[...], wqu[:, columns]) + b_qkv[:, columns]
        if kind < 2:
            part = turn(part, forth)
        qkv[:, columns] = part.astype(LOW)
    done(1)
    masks = head_masks(LOW)
    heads = len(masks)
    for r in range(GROUP):
        here = slice(r * rows, (r + 1) * rows)
        query, keys, values = [qkv[here, k * SIDE : (k + 1) * SIDE] for k in range(3)]
        stacked = jnp.concatenate([query * m for m in masks], axis=0)
        scores = dot_cols(stacked, keys) * HEAD_DIM ** (-0.5)
        scores = scores.reshape(heads, rows, rows) + mask[here, :][None]
        expo = jnp.exp(scores - jnp.max(scores, axis=-1, keepdims=True))
        prob = expo / jnp.sum(expo, axis=-1, keepdims=True)
        prob = prob.reshape(heads * rows, rows)
        probs[r * heads * rows : (r + 1) * heads * rows, :] = prob
        full = dot(prob.astype(LOW), values)
        mixed[here, :] = by_head([full[h * rows : (h + 1) * rows] for h in range(heads)]).astype(LOW)
    done(2)
    done(3)
    tile = 256
    for at in range(0, UNITS, tile):
        hidden = dot(y[...], wqu[:, 3 * SIDE + at : 3 * SIDE + at + tile]) + b_up[:, at : at + tile]
        share = 0.5 * (1.0 + lax.erf(hidden * (0.5**0.5)))
        density = jnp.exp(-0.5 * hidden * hidden) * (0.5 / jnp.pi) ** 0.5
        active[:, at : at + tile] = (hidden * share).astype(LOW)
        slope[:, at : at + tile] = share + hidden * density
    done(4)
    done(5)
    waits[1]()
    for at in range(0, D, tile):
        branch = dot(mixed[...], wout[:, at : at + tile]) + dot(active[...], wdown[:, at : at + tile])
        for r in range(GROUP):
            z_refs[r][:, at : at + tile] = branch[r * rows : (r + 1) * rows].astype(LOW)


def backward_part(grad, normed, tables, wqu, wout, wdown, kept, dqu, dy_refs, sums, waits, done):
    cosine, sine, _ = tables
    y, qkv, probs, mixed, active, slope = kept
    rows = grad.shape[0] // GROUP
    tile = 256
    waits[0]()
    dmixed = dot_cols(grad[...], wout[...]).astype(LOW)
    for at in range(0, UNITS, tile):
        dactive = dot_cols(grad[...], wdown[at : at + tile, :])
        dhidden = (dactive * slope[:, at : at + tile]).astype(LOW)
        dqu[:, 3 * SIDE + at : 3 * SIDE + at + tile] = dhidden
    waits[1]()
    masks = head_masks(LOW)
    heads = len(masks)
    back = turning(cosine[...], sine[...], True)
    for r in range(GROUP):
        here = slice(r * rows, (r + 1) * rows)
        query, keys, values = [qkv[here, k * SIDE : (k + 1) * SIDE] for k in range(3)]
        dstack = jnp.concatenate([dmixed[here] * m for m in masks], axis=0)
        dprob = dot_cols(dstack, values)
        prob = probs[r * heads * rows : (r + 1) * heads * rows, :]
        dvalues = dot_rows(prob.astype(LOW), dstack)
        dscore = (prob * (dprob - jnp.sum(prob * dprob, axis=-1, keepdims=True))).astype(LOW)
        full = dot(dscore, keys)
        dquery = by_head([full[h * rows : (h + 1) * rows] for h in range(heads)])
        dkeys = dot_rows(dscore, jnp.concatenate([query * m for m in masks], axis=0))
        scale = HEAD_DIM ** (-0.5)
        slot_tables = [a[here] for a in back]
        dqu[here, 0:SIDE] = turn(dquery * scale, slot_tables).astype(LOW)
        dqu[here, SIDE : 2 * SIDE] = turn(dkeys * scale, slot_tables).astype(LOW)
        dqu[here, 2 * SIDE : 3 * SIDE] = dvalues.astype(LOW)
    done()
    for at in range(0, MIXED, tile):
        sums[:, at : at + tile] = jnp.sum(dqu[:, at : at + tile].astype(F32), axis=0, keepdims=True)
    waits[2]()
    for at in range(0, D, tile):
        dy = dot_cols(dqu[...], wqu[at : at + tile, :])
        for r in range(GROUP):
            dy_refs[r][:, at : at + tile] = dy[r * rows : (r + 1) * rows].astype(LOW)
        own = grad[0:rows, at : at + tile].astype(F32)
        for i, terms in enumerate((own, dy * normed[:, at : at + tile], dy)):
            begin = MIXED + i * D + at
            sums[:, begin : begin + tile] = jnp.sum(terms, axis=0, keepdims=True)


def kept_shapes(tokens, rows):
    return [
        ((tokens, D), LOW),
        ((tokens, 3 * SIDE), LOW),
        ((tokens * (SIDE // HEAD_DIM), rows), F32),
        ((tokens, SIDE), LOW),
        ((tokens, UNITS), LOW),
        ((tokens, UNITS), F32),
    ]


def weight_scratch():
    return [
        pltpu.VMEM((D, MIXED), LOW),
        pltpu.VMEM((SIDE, D), LOW),
        pltpu.VMEM((UNITS, D), LOW),
        pltpu.SemaphoreType.DMA((2,)),
    ]


def waiter(copies):
    def wait():
        for copy in copies:
            copy.wait()

    return wait


def started(pairs, sem):
    copies = [pltpu.make_async_copy(source, target, sem) for source, target in pairs]
    for copy in copies:
        copy.start()
    return waiter(copies)


def table_scratch(tokens, rows):
    return [pltpu.VMEM((tokens, 128), F32), pltpu.VMEM((tokens, 128), F32), pltpu.VMEM((tokens, rows), F32)]


def cost(flops, moved):
    return pl.CostEstimate(flops=2 * flops, bytes_accessed=2 * moved, transcendentals=0)


def leaving(pairs, sems):
    copies = [pltpu.make_async_copy(near, far, sems.at[i]) for i, (near, far) in enumerate(pairs)]

    def go(i):
        copies[i].start()

    return go, waiter(copies)


def pair_copies(info, slots, keep, send, sems):
    targets = (keep.at[0], keep.at[1], send.at[0], send.at[1])
    return [
        [pltpu.make_async_copy(slots[r], target, sems.at[i]) for i, (r, target) in enumerate(zip(order, targets))]
        for order in ((0, 2, 1, 3), (0, 1, 2, 3))
    ]


def on_core(info, copies, act):
    for here in range(2):

        @pl.when(info[0] == here)
        def _(mine=copies[here]):
            for copy in mine:
                act(copy)


def forward_kernel(ring, count, info, *refs):
    parts, refs = refs[:count], refs[count:]
    x_refs, refs = refs[:4], refs[4:]
    tables, refs = refs[:3], refs[3:]
    vecs, refs = refs[:4], refs[4:]
    z_refs, refs = refs[:4], refs[4:]
    far_kept, far_weights, far_tables, refs = refs[:7], refs[7:10], refs[10:13], refs[13:]
    kept, refs = refs[:7], refs[7:]
    out_sems, scratch = refs[0], refs[1:]
    weights = scratch[:3]
    qu_copies, od_copies = weight_copies(ring, info, parts, *scratch)
    for copy in qu_copies + od_copies:
        copy.start()
    pairs = [*zip(kept, far_kept), *zip(weights, far_weights), *zip(tables, far_tables)]
    go, out = leaving(pairs, out_sems)
    for i in range(10, 13):
        go(i)

    def qu_in():
        waiter(qu_copies)()
        go(7)

    def od_in():
        waiter(od_copies)()
        go(8)
        go(9)

    def done(i):
        go(i)
        if i == 0:
            go(6)

    forward_part(x_refs, tables, vecs, *weights, kept[:6], z_refs, (qu_in, od_in, no_wait), done, kept[6])
    out()


def forward(ring, info, parts, xs, tables, vecs, rows):
    tokens = GROUP * rows
    shapes = kept_shapes(tokens, rows) + [((tokens, D), F32)]
    away = [*shapes, ((D, MIXED), LOW), ((SIDE, D), LOW), ((UNITS, D), LOW)] + [(a.shape, F32) for a in tables]
    blocks = (*xs, *tables, *vecs)
    return pl.pallas_call(
        functools.partial(forward_kernel, ring, len(parts)),
        out_shape=(*[shaped((rows, D), LOW)] * GROUP, *[pltpu.HBM(*a) for a in away]),
        in_specs=[smem_spec()] + [any_spec()] * len(parts) + [full_spec(a.shape) for a in blocks],
        out_specs=tuple([full_spec((rows, D))] * GROUP + [far_spec()] * len(away)),
        scratch_shapes=[pltpu.VMEM(*a) for a in shapes]
        + [pltpu.SemaphoreType.DMA((len(away),))]
        + weight_scratch(),
        compiler_params=kernel_params(22),
        cost_estimate=cost(2 * tokens * D * (D + 2 * FF // GROUP), 16 * 1024 * 1024),
        name="forward_shard",
    )(info, *parts, *blocks)


def middle_kernel(ring, count, info, *refs):
    parts, refs = refs[:count], refs[count:]
    x_refs, refs = refs[:4], refs[4:]
    g_refs, refs = refs[:4], refs[4:]
    far_tables, refs = refs[:3], refs[3:]
    vecs, refs = refs[:4], refs[4:]
    dy_refs, refs = refs[:4], refs[4:]
    sums, away, (z_keep, z_send), refs = refs[0], refs[1:6], refs[6:8], refs[8:]
    kept, refs = refs[:6], refs[6:]
    z_refs, tables, refs = refs[:4], refs[4:7], refs[7:]
    (grad, normed, dqu, in_sems, out_sems, z_sems), scratch = refs[:6], refs[6:]
    rows = z_refs[0].shape[0]
    qu_copies, od_copies = weight_copies(ring, info, parts, *scratch)
    for copy in qu_copies:
        copy.start()
    tables_in = started(zip(far_tables, tables), in_sems.at[0])
    for copy in od_copies:
        copy.start()
    pairs = []
    for r, ref in enumerate(g_refs):
        at = ref.shape[0] - rows
        pairs.append((ref.at[pl.ds(at, rows)], grad.at[pl.ds(r * rows, rows)]))
    grad_in = started(pairs, in_sems.at[1])
    go, out = leaving(list(zip([kept[0], kept[3], kept[4], dqu, grad], away)), out_sems)

    def done(i):
        if i in (0, 3, 4):
            go((0, 3, 4).index(i))

    waits = (waiter(qu_copies), waiter(od_copies), tables_in)
    forward_part(x_refs, tables, vecs, *scratch[:3], kept, z_refs, waits, done, normed)
    grad_in()
    go(4)
    z_copies = pair_copies(info, z_refs, z_keep, z_send, z_sems)
    on_core(info, z_copies, lambda copy: copy.start())
    waits = (no_wait, no_wait, no_wait)
    done = functools.partial(go, 3)
    backward_part(grad, normed, tables, *scratch[:3], kept, dqu, dy_refs, sums, waits, done)
    out()
    on_core(info, z_copies, lambda copy: copy.wait())


def middle(ring, info, parts, xs, gs, tables, vecs, rows):
    tokens = GROUP * rows
    shapes = kept_shapes(tokens, rows)
    away = [shapes[0], shapes[3], shapes[4], ((tokens, MIXED), LOW), ((tokens, D), LOW)]
    away += [((2, rows, D), LOW)] * 2
    sums = shaped((1, MIXED + 3 * D), F32)
    return pl.pallas_call(
        functools.partial(middle_kernel, ring, len(parts)),
        out_shape=(*[shaped((rows, D), LOW)] * GROUP, sums, *[pltpu.HBM(*a) for a in away]),
        in_specs=[smem_spec()]
        + [any_spec()] * len(parts)
        + [full_spec(a.shape) for a in xs]
        + [far_spec()] * (GROUP + 3)
        + [full_spec(a.shape) for a in vecs],
        out_specs=tuple([full_spec((rows, D))] * GROUP + [full_spec(sums.shape)] + [far_spec()] * len(away)),
        scratch_shapes=[pltpu.VMEM(*a) for a in shapes]
        + [pltpu.VMEM((rows, D), LOW)] * GROUP
        + table_scratch(tokens, rows)
        + [pltpu.VMEM((tokens, D), LOW), pltpu.VMEM((tokens, D), F32), pltpu.VMEM((tokens, MIXED), LOW)]
        + [pltpu.SemaphoreType.DMA((2,)), pltpu.SemaphoreType.DMA((5,)), pltpu.SemaphoreType.DMA((4,))]
        + weight_scratch(),
        compiler_params=kernel_params(27),
        cost_estimate=cost(4 * tokens * D * (D + 2 * FF // GROUP), 16 * 1024 * 1024),
        name="forward_backward_shard",
    )(info, *parts, *xs, *[far(a) for a in (*gs, *tables)], *vecs)


def backward_kernel(ring, info, *refs):
    g_refs, refs = refs[:4], refs[4:]
    far_kept, far_weights, far_tables, refs = refs[:7], refs[7:10], refs[10:13], refs[13:]
    (dy_keep, dy_send, keep, send), refs = refs[:4], refs[4:]
    kept, refs = refs[:7], refs[7:]
    weights, tables, refs = refs[:3], refs[3:6], refs[6:]
    (grad, dqu, sums, in_sems, out_sems), dy_refs = refs[:5], refs[5:]
    y, qkv, probs, mixed, active, slope, normed = kept
    wqu, wout, wdown = weights
    far_y, far_qkv, far_probs, far_mixed, far_active, far_slope, far_normed = far_kept
    mixed_in = started([(far_mixed, mixed)], in_sems.at[0])
    active_in = started([(far_active, active)], in_sems.at[1])
    units_in = started([*zip(far_weights[1:], weights[1:]), (far_slope, slope)], in_sems.at[2])
    heads_in = started([(far_qkv, qkv), (far_probs, probs), *zip(far_tables, tables)], in_sems.at[3])
    dy_in = started([(far_weights[0], wqu), (far_normed, normed)], in_sems.at[4])
    y_in = started([(far_y, y)], in_sems.at[5])
    rows = g_refs[0].shape[0]
    for r in range(GROUP):
        grad[r * rows : (r + 1) * rows, :] = g_refs[r][...]
    mixed_in()
    od_part(ring, info, mixed, active, grad, keep, send, active_in)
    waits = (units_in, heads_in, dy_in)
    backward_part(grad, normed, tables, *weights, kept[:6], dqu, dy_refs, sums, waits, no_wait)
    copies = pair_copies(info, dy_refs, dy_keep, dy_send, out_sems)
    on_core(info, copies, lambda copy: copy.start())
    y_in()
    qu_part(ring, info, y, dqu, sums, keep, send)
    on_core(info, copies, lambda copy: copy.wait())


def backward(ring, info, gs, held, rows):
    tokens = GROUP * rows
    outs = [shaped((2, rows, D), LOW)] * 2 + [grads_shape(ring)] * 2
    return pl.pallas_call(
        functools.partial(backward_kernel, ring),
        out_shape=tuple(outs),
        in_specs=[smem_spec()] + [full_spec(a.shape) for a in gs] + [far_spec()] * len(held),
        out_specs=tuple(full_spec(a.shape) for a in outs),
        scratch_shapes=[pltpu.VMEM(a.shape, a.dtype) for a in held]
        + [pltpu.VMEM((tokens, D), LOW), pltpu.VMEM((tokens, MIXED), LOW)]
        + [pltpu.VMEM((1, MIXED + 3 * D), F32), pltpu.SemaphoreType.DMA((6,)), pltpu.SemaphoreType.DMA((4,))]
        + [pltpu.VMEM((rows, D), LOW)] * GROUP,
        compiler_params=kernel_params(28),
        cost_estimate=cost(4 * tokens * D * (D + 2 * FF // GROUP), 16 * 1024 * 1024),
        name="backward_shard",
    )(info, *gs, *[far(a) for a in held])


def slot_in(ring, difference, half):
    straight, turned = ring.slot(difference, 0), ring.slot(difference, 1)
    return straight + half * (turned - straight)


QU_TILES = PART // 128
OD_TILES = D // 2 // 128
SIDES = 112


def slot_rows(ring):
    return GROUP * QU_TILES * (D // ring.count) + OD_TILES * (SIDE + UNITS) // ring.size


def grads_shape(ring):
    return shaped((ring.size * slot_rows(ring) + SIDES, 128), LOW)


def od_part(ring, info, mixed, active, grad, keep, send, active_in):
    core, spot = info[0], info[2]
    out_rows = SIDE // ring.size
    ff_rows = UNITS // ring.size
    ahead = GROUP * QU_TILES * (D // ring.count)
    for i, (out, half) in enumerate(((send, 1 - core), (keep, core))):
        columns = pl.ds(pl.multiple_of(half * (D // 2), D // 2), D // 2)
        part = grad[:, columns]
        block = dot_rows(mixed[...], part).astype(LOW)
        if i == 0:
            active_in()
        for there in range(ring.size):
            slot = slot_in(ring, spot ^ there, half)
            piece = dot_rows(active[:, there * ff_rows : (there + 1) * ff_rows], part).astype(LOW)
            for tile in range(OD_TILES):
                lanes = slice(tile * 128, (tile + 1) * 128)
                row = slot * slot_rows(ring) + ahead + tile * (ff_rows + out_rows)
                out[pl.ds(pl.multiple_of(row, 16), ff_rows), :] = piece[:, lanes]
                row = pl.multiple_of(row + ff_rows, 16)
                out[pl.ds(row, out_rows), :] = block[there * out_rows : (there + 1) * out_rows, lanes]


def vector_rows(group, sums):
    width = SIDE // SPREAD
    run = UNITS // SPREAD
    row = lax.broadcasted_iota(jnp.int32, (SIDES, 128), 0)
    pieces = []
    for at in range(0, 3 * SIDE, 128):
        pieces.append(((at // width * GROUP + group) * (width // 128) + at % width // 128, at))
    for at in range(0, UNITS, 128):
        pieces.append((3 * D // 128 + D // 128 + (at // run * GROUP + group) * (run // 128) + at % run // 128, 3 * SIDE + at))
    tail = (4 * D + FF) // 128
    for i, begin in enumerate((3 * D // 128, tail, tail + D // 128, tail + 2 * D // 128)):
        for at in range(0, D, 128):
            pieces.append((begin + at // 128, MIXED + max(i - 1, 0) * D + at))
    return sum(jnp.where(row == where, sums[:, at : at + 128], 0.0) for where, at in pieces)


def qu_part(ring, info, y, dqu, sums, keep, send):
    core, group, spot = info[0], info[1], info[2]
    rows = D // ring.count
    tile = 256
    last = ring.size * slot_rows(ring)
    extra = vector_rows(group, sums).astype(LOW)
    for out, half in ((send, 1 - core), (keep, core)):
        columns = pl.ds(pl.multiple_of(half * PART, 128), PART)
        out[last : last + SIDES, :] = extra
        for at in range(0, D, tile):
            block = dot_rows(y[:, at : at + tile], dqu[:, columns]).astype(LOW)
            for offset in range(0, tile, rows):
                dp = (at + offset) // rows
                slot = slot_in(ring, spot ^ ring.spot_of(dp), half)
                begin = slot * slot_rows(ring) + (group ^ ring.group_of(dp)) * (QU_TILES * rows)
                for i in range(QU_TILES):
                    row = pl.multiple_of(begin + i * rows, 16)
                    out[pl.ds(row, rows), :] = block[offset : offset + rows, i * 128 : (i + 1) * 128]


def grads_kernel(ring, info, far_mixed, far_active, far_grad, far_y, far_dqu, sums, keep, send, *scratch):
    mixed, active, grad, y, dqu, sems = scratch
    grad_in = started([(far_grad, grad), (far_mixed, mixed)], sems.at[0])
    active_in = started([(far_active, active)], sems.at[1])
    rest_in = started([(far_y, y), (far_dqu, dqu)], sems.at[2])
    grad_in()
    od_part(ring, info, mixed, active, grad, keep, send, active_in)
    rest_in()
    qu_part(ring, info, y, dqu, sums, keep, send)


def weight_grads(ring, info, mixed, active, grad, y, dqu, sums):
    blocks = (mixed, active, grad, y, dqu)
    out = grads_shape(ring)
    return pl.pallas_call(
        functools.partial(grads_kernel, ring),
        out_shape=(out, out),
        in_specs=[smem_spec()] + [far_spec()] * len(blocks) + [full_spec(sums.shape)],
        out_specs=(full_spec(out.shape),) * 2,
        scratch_shapes=[pltpu.VMEM(a.shape, LOW) for a in blocks] + [pltpu.SemaphoreType.DMA((3,))],
        compiler_params=kernel_params(20),
        cost_estimate=cost(50 * 10**9, 12 * 1024 * 1024),
        name="weight_grads",
    )(info, *[far(a) for a in blocks], sums)


def fold_kernel(held, came, kept, sent):
    half = (held.shape[0] - SIDES) // 2
    full = 2 * half
    kept[0:half, :] = held[0:half, :].astype(F32) + came[0:half, :].astype(F32)
    sent[0:half, :] = (held[half:full, :].astype(F32) + came[half:full, :].astype(F32)).astype(LOW)
    sides = held[full : full + SIDES, :].astype(LOW).astype(F32) + came[full : full + SIDES, :].astype(F32)
    kept[half : half + SIDES, :] = sides
    sent[half : half + SIDES, :] = sides.astype(LOW)


def fold(held, came):
    half = (held.shape[0] - SIDES) // 2 + SIDES
    outs = (shaped((half, 128), F32), shaped((half, 128), LOW))
    return pl.pallas_call(
        fold_kernel,
        out_shape=outs,
        in_specs=[full_spec(held.shape), full_spec(came.shape)],
        out_specs=tuple(full_spec(a.shape) for a in outs),
        compiler_params=kernel_params(20),
        cost_estimate=cost(0, 1024 * 1024),
        name="fold_gradients",
    )(held, came)


VECTOR_ROWS = (7 * D + FF) // 128


def close_kernel(held, came, before, *outs):
    qus, od, squares = outs[:GROUP], outs[GROUP], outs[GROUP + 1]
    rows = qus[0].shape[0] - SIDES
    full = held.shape[0] - SIDES
    sides = held[full : full + SIDES, :].astype(LOW).astype(F32) + came[full : full + SIDES, :].astype(F32)
    lanes = before[...]
    begin = 0
    for piece in (*qus, od):
        length = rows if piece is not od else od.shape[0]
        here = slice(begin, begin + length)
        begin += length
        total = held[here, :].astype(F32) + came[here, :].astype(F32)
        piece[0:length, :] = total.astype(LOW)
        lanes = lanes + jnp.sum((total * total).reshape(length // 8, 8, 128), axis=0)
    squares[...] = lanes
    high = lanes.astype(LOW).astype(F32)
    rest = sides[VECTOR_ROWS + 16 :]
    sides = jnp.concatenate([sides[:VECTOR_ROWS], high, lanes - high, rest], axis=0).astype(LOW)
    for piece in qus:
        piece[rows : rows + SIDES, :] = sides


def close(ring, held, came, before):
    rows = QU_TILES * (D // ring.count)
    outs = [shaped((rows + SIDES, 128), LOW)] * GROUP
    outs += [shaped((OD_TILES * (SIDE + UNITS) // ring.size, 128), LOW), shaped((8, 128), F32)]
    return pl.pallas_call(
        close_kernel,
        out_shape=tuple(outs),
        in_specs=[full_spec(held.shape), full_spec(came.shape), full_spec(before.shape)],
        out_specs=tuple(full_spec(a.shape) for a in outs),
        compiler_params=kernel_params(16),
        cost_estimate=cost(0, 1024 * 1024),
        name="close_gradients",
    )(held, came, before)


def join_kernel(info, *refs):
    core = info[0]
    firsts, seconds, (od_first, od_second), outs = refs[:4], refs[4:8], refs[8:10], refs[10:]
    sent, vec, squares, vec_squares = outs
    rows = firsts[0].shape[0] - SIDES
    sides = []
    for pieces in (firsts, seconds):
        parts = [a[rows : rows + SIDES, :].astype(F32) for a in pieces]
        sides.append((parts[0] + parts[1]) + (parts[2] + parts[3]))
    squares[...] = sides[0][VECTOR_ROWS : VECTOR_ROWS + 8] + sides[0][VECTOR_ROWS + 8 : VECTOR_ROWS + 16]
    own = [(a[:VECTOR_ROWS] * a[:VECTOR_ROWS]).reshape(VECTOR_ROWS // 8, 8, 128) for a in sides]
    vec_squares[...] = jnp.sum(own[0], axis=0) + jnp.sum(own[1], axis=0)
    vec[...] = jnp.where(core == 0, sides[0], sides[1])

    def write(pieces, od):
        for r in range(GROUP):
            sent[r * rows : (r + 1) * rows, :] = pieces[r][0:rows, :]
        sent[GROUP * rows :, :] = od[...]

    pl.when(core == 0)(functools.partial(write, seconds, od_second))
    pl.when(core == 1)(functools.partial(write, firsts, od_first))


def join(info, firsts, seconds, od_first, od_second):
    rows = firsts[0].shape[0] - SIDES
    outs = (shaped((GROUP * rows + od_first.shape[0], 128), LOW), shaped((SIDES, 128), F32))
    outs += (shaped((8, 128), F32),) * 2
    blocks = (*firsts, *seconds, od_first, od_second)
    return pl.pallas_call(
        join_kernel,
        out_shape=outs,
        in_specs=[smem_spec()] + [full_spec(a.shape) for a in blocks],
        out_specs=tuple(full_spec(a.shape) for a in outs),
        compiler_params=kernel_params(16),
        cost_estimate=cost(0, 1024 * 1024),
        name="join_members",
    )(info, *blocks)


def adam_update(weight, grad, first, second, factor, rate):
    clipped = grad * factor
    first_new = BETA_ONE * first + (1.0 - BETA_ONE) * clipped
    second_new = BETA_TWO * second + (1.0 - BETA_TWO) * clipped * clipped
    first_hat = first_new / (1.0 - BETA_ONE**STEP)
    second_hat = second_new / (1.0 - BETA_TWO**STEP)
    weight_new = weight - rate * (
        first_hat / (jnp.sqrt(second_hat) + ADAM_EPS) + WEIGHT_DECAY * weight
    )
    return (weight_new, first_new, second_new)


def mixed_tile(tile, member):
    at = tile * 128
    if at >= 3 * SIDE:
        return 2, up_column(member, at - 3 * SIDE)
    width = SIDE // SPREAD
    kind, within = at // SIDE, at % SIDE
    return 0, qkv_column(kind, within // width, member) + within % width


def adam_kernel(info, factor_ref, *refs):
    core, group = info[0], info[1]
    step = pl.program_id(0)
    factor = factor_ref[0]
    qus, refs = (refs[:4], refs[4:8]), refs[8:]
    ods, came, refs = refs[:2], refs[2], refs[3:]
    olds, news = refs[:12], refs[12:]
    few, many = olds[0].shape[1], olds[9].shape[1]
    rows = (qus[0][0].shape[0] - SIDES) // QU_TILES
    od_rows = ods[0].shape[0] // OD_TILES

    def update(which, column, grad):
        columns = slice(column, column + 128)
        weight, first, second = [olds[3 * which + i][0, :, columns] for i in range(3)]
        fresh = adam_update(weight, grad.astype(F32), first, second, factor, LEARN_RATE)
        for i in range(3):
            news[3 * which + i][0, :, columns] = fresh[i]

    def rows_of(ref, begin, length):
        return ref[pl.ds(pl.multiple_of(begin + step * length, 16), length), :]

    def both_halves(here):
        for half in range(2):
            for tile in range(OD_TILES):
                column = half * (D // 2) + tile * 128
                ref, begin = (ods[here], 0) if half == here else (came, GROUP * QU_TILES * rows)
                begin = begin + tile * od_rows
                update(3, column, rows_of(ref, begin, many))
                update(1, column, rows_of(ref, begin + od_rows - rows, few))
            for member in range(GROUP):
                if half == here:
                    for g in range(GROUP):

                        @pl.when(group == g)
                        def _(ref=qus[here][member ^ g]):
                            for tile in range(QU_TILES):
                                which, column = mixed_tile(half * QU_TILES + tile, member)
                                update(which, column, rows_of(ref, tile * rows, few))
                else:
                    for tile in range(QU_TILES):
                        which, column = mixed_tile(half * QU_TILES + tile, member)
                        begin = ((group ^ member) * QU_TILES + tile) * rows
                        update(which, column, rows_of(came, begin, few))

    for here in range(2):
        pl.when(core == here)(functools.partial(both_halves, here))


def adam(info, factor, qus, ods, came, olds):
    steps = max(1, olds[0].shape[1] // 16)

    def master(a):
        return pl.BlockSpec((1, a.shape[1] // steps, a.shape[2]), lambda i: (0, i, 0))

    grads = (*qus[0], *qus[1], *ods, came)
    return pl.pallas_call(
        adam_kernel,
        grid=(steps,),
        out_shape=tuple(shaped(a.shape, F32) for a in olds),
        in_specs=[smem_spec(), smem_spec()]
        + [full_spec(a.shape) for a in grads]
        + [master(a) for a in olds],
        out_specs=tuple(master(a) for a in olds),
        compiler_params=kernel_params(28),
        name="adamw",
    )(info, factor, *grads, *[far(a) for a in olds])


def doc_tables(lengths, rows):
    seqs = lengths.shape[0]
    ends = jnp.cumsum(lengths, axis=1)
    places = jnp.arange(rows, dtype=jnp.int32)
    past = places[None, :, None] >= ends[:, None, :]
    begins = jnp.sum(jnp.where(past, lengths[:, None, :], 0), axis=2)
    position = (places[None, :] - begins).reshape(seqs * rows, 1)
    half = ROT // 2
    inverse = 10000.0 ** (-(jnp.arange(half, dtype=F32) * 2.0) / ROT)
    lanes = jnp.concatenate([inverse, inverse, jnp.zeros(HEAD_DIM - ROT, F32)])
    angles = position.astype(F32) * jnp.concatenate([lanes, lanes])[None, :]
    allowed = (places[None, None, :] <= places[None, :, None]) & (places[None, None, :] >= begins[:, :, None])
    mask = jnp.where(allowed, 0.0, -1e30).reshape(seqs * rows, rows).astype(F32)
    return jnp.cos(angles), jnp.sin(angles), mask


def shards(
    x_in,
    cotangent,
    doc_lengths,
    w_qkv,
    w_out,
    w_up,
    w_down,
    vectors,
    m_qkv,
    m_out,
    m_up,
    m_down,
    m_vectors,
    v_qkv,
    v_out,
    v_up,
    v_down,
    v_vectors,
):
    place = Place()
    ring, core, group, spot = place.ring, place.core, place.group, place.spot
    info = place.info()
    local_rows, width = x_in.shape
    seqs, docs = doc_lengths.shape
    rows = local_rows // seqs
    in_rows = w_qkv.shape[1]
    shard = vectors.shape[1]
    members = range(1, GROUP)

    vec_block = jnp.pad(vectors[0].astype(LOW), (0, 8 * 128 - shard)).reshape(8, 128)
    vec_block = jnp.pad(jnp.concatenate([vec_block, vec_block]), ((0, in_rows - 16), (0, 0)))
    keep_qu, send_qu, keep_od, send_od = pack(info, w_qkv, w_out, w_up, w_down, vec_block)
    came_qu = place.sibling(send_qu)
    came_od = place.sibling(send_od)

    def member_columns():
        row = jnp.arange(in_rows)[None, :, None]
        later = (row >= 8) & (row < 16) & (jnp.arange(WIRE)[None, None, :] >= PART)
        qu = jnp.where((core == 0) ^ later, keep_qu, came_qu)
        return [take(qu, group)] + [place.member(take(qu, group ^ r), r) for r in members]

    def gather(block, *waited):
        late = after(block, *waited)
        return [block] + [place.member(late, r) for r in members]

    def to_owners(slots):
        return [slots[0]] + [place.member(slots[r], r) for r in members]

    def total_of(slots):
        return sum(a.astype(F32) for a in slots)

    def both_vectors(parts):
        pieces = jnp.concatenate([a[:, :, 0:16, PART:] for a in parts])
        pieces = pieces.reshape(ring.size * GROUP, 2, 8 * 128)[:, :, :shard]
        dp = jnp.arange(ring.count, dtype=jnp.int32)
        difference = ring.spot_of(dp) ^ spot
        slot = jnp.where(core == 0, ring.slot(difference, 0), ring.slot(difference, 1))
        vec = jnp.take(pieces, slot * GROUP + (ring.group_of(dp) ^ group), axis=0, mode="clip")
        return [block_vectors(vec[:, block].reshape(-1).astype(F32)) for block in range(2)]

    def block_vectors(vec):
        b_qkv, b_out, b_up, b_down, gain, ln_bias = jnp.split(
            vec, [3 * D, 4 * D, 4 * D + FF, 5 * D + FF, 6 * D + FF]
        )
        b_qkv = take(b_qkv.reshape(3 * SPREAD, GROUP, -1), group, 1).reshape(1, -1)
        b_up = take(b_up.reshape(SPREAD, GROUP, -1), group, 1).reshape(1, -1)
        return (b_qkv, b_up, gain[None], ln_bias[None]), (b_out + b_down)[None], gain[None]

    x_own = take(x_in.reshape(2, rows, width), core)
    cot_own = take(cotangent.reshape(2, rows, width), core)
    len_own = take(doc_lengths, core)
    len_rows = jnp.zeros((16, width), LOW).at[0, :docs].set(len_own.astype(LOW))
    x_sent = jnp.concatenate([x_own, len_rows])

    qu_came = member_columns()
    qu_own = jnp.stack(qu_came)[None]
    x_near = [place.member(after(x_sent, qu_came[1]), r) for r in (1, 2)]
    x_group = [x_sent, *x_near]
    od_own = jnp.where(core == 0, keep_od, came_od)[None]
    od = [jnp.concatenate([od_own, place.across(od_own, 0)])]
    qu_own = after(qu_own, od[0])
    qu = [jnp.concatenate([qu_own, place.across(qu_own, 0)])]
    x_group.append(place.member(after(x_near[1], qu[0], od[0]), 1))
    qu_sibling = [place.sibling(qu[0])]
    od_sibling = [place.sibling(od[0])]
    for step in range(1, ring.bits):
        od.append(place.across(jnp.concatenate(od), step))
        qu.append(place.across(after(jnp.concatenate(qu), od[-1]), step))
    qu_sibling += [place.sibling(a) for a in qu[1:]]
    od_sibling += [place.sibling(a) for a in od[1:]]
    qu_mine = jnp.where(core == 1, keep_qu, came_qu)
    waited = (*x_group[1:], qu_sibling[0], od_sibling[0])
    sent = [after(jnp.concatenate([take(qu_mine, group ^ r), cot_own]), *waited) for r in members]
    qu_cot = [place.member(a, r) for a, r in zip(sent, members)]
    parts_first = (*qu, *od, *qu_sibling, *od_sibling)
    lengths = jnp.stack([a[rows, :docs] for a in x_group]).astype(jnp.int32)
    tables = doc_tables(lengths, rows)
    (vecs_first, bias_first, gain_first), (vecs_second, bias_second, gain_second) = both_vectors(qu)

    first = forward(ring, info, parts_first, x_group, tables, vecs_first, rows)
    kept_first, tables = first[GROUP:], first[-3:]
    qu_cot = [after(a, first[0]) for a in qu_cot]
    came = to_owners(first[:GROUP])
    od_own = after(jnp.where(core == 1, keep_od, came_od)[None], first[0])
    od_late = [jnp.concatenate([od_own, place.across(od_own, 0)])]
    came[1] = after(came[1], od_late[0])
    came[2] = after(came[2], *vecs_second, bias_second, gain_second)
    hidden_first = (x_own.astype(F32) + total_of(came) + bias_first).astype(LOW)
    hidden_group = gather(hidden_first)
    qu_own = jnp.stack([take(qu_mine, group)] + [a[:in_rows] for a in qu_cot])[None]
    qu_late = [jnp.concatenate([qu_own, after(place.across(qu_own, 0), hidden_first)])]
    for step in range(1, ring.bits):
        od_late.append(after(place.across(jnp.concatenate(od_late), step), *hidden_group[1:]))
        qu_late.append(after(place.across(jnp.concatenate(qu_late), step), *hidden_group[1:]))
    qu_sibling, od_sibling = [
        [place.sibling(after(a, *hidden_group[1:])) for a in late] for late in (qu_late, od_late)
    ]
    parts_second = (*qu_late, *od_late, *qu_sibling, *od_sibling)
    second = middle(ring, info, parts_second, hidden_group, [cot_own, *qu_cot], tables, vecs_second, rows)
    sums_second, y_second, mixed_second, active_second, dqu_second, grad_second = second[GROUP : GROUP + 6]
    z_keep, z_send = second[GROUP + 6 :]

    def rows_backward(rows_low, grad_low, dy, gain):
        rows_now = rows_low.astype(F32)
        centered = rows_now - jnp.mean(rows_now, axis=-1, keepdims=True)
        variance = jnp.mean(centered * centered, axis=-1, keepdims=True)
        inverse_std = lax.rsqrt(variance + NORM_EPS)
        normed = centered * inverse_std
        scaled = dy * gain
        inner_mean = jnp.mean(scaled, axis=-1, keepdims=True)
        inner_cross = jnp.mean(scaled * normed, axis=-1, keepdims=True)
        return (grad_low.astype(F32) + inverse_std * (scaled - inner_mean - normed * inner_cross)).astype(LOW)

    def to_members(pieces):
        return [pieces[0]] + [place.member(pieces[r], r) for r in members]

    steps = list(reversed(range(ring.bits)))

    def ring_fold(held, *waited):
        kept, sent = held
        for step in steps[:-1]:
            kept, sent = fold(kept, after(place.across(sent, step), *waited))
        return kept, sent

    dy_second = to_owners(second[:GROUP])
    grads = weight_grads(ring, info, mixed_second, active_second, grad_second, y_second, dqu_second, sums_second)
    mid_grad = rows_backward(hidden_first, cot_own, total_of(dy_second), gain_second)
    mid_group = gather(mid_grad)
    sent = place.sibling(after(grads[1], *dy_second[1:]))
    second_held = ring_fold(fold(grads[0], after(sent, mid_grad)))

    mid_late = [after(mid_group[0], *second_held)] + mid_group[1:]
    z_came = place.toward(after(z_send, *mid_group[1:]), 1)
    dy_keep, dy_send, keep, send = backward(ring, info, mid_late, kept_first, rows)
    z_came = after(z_came, send)
    kept, sent = second_held
    none = jnp.zeros((8, 128), F32)
    *qu_second, od_second, squares_second = close(ring, kept, after(place.across(sent, 0), send), none)
    send = after(send, *qu_second, z_came)
    qu_slots_second = to_members(qu_second)
    kept, sent = ring_fold(fold(keep, place.sibling(send)))
    dy_came = place.toward(after(dy_send, *qu_slots_second[1:]), 1)
    z_step = place.toward((z_keep[1].astype(F32) + z_came[1].astype(F32)).astype(LOW), 0)
    came = after(place.across(after(sent, *qu_slots_second[1:], z_step), 0), dy_came)
    *qu_first, od_first, _ = close(ring, kept, came, squares_second)
    qu_slots_first = to_members(qu_first)
    dy_step = (dy_keep[1].astype(F32) + dy_came[1].astype(F32)).astype(LOW)
    dy_step = place.toward(after(dy_step, *qu_slots_first[1:]), 0)
    grads_sent, vec, squares, vec_squares = join(info, qu_slots_first, qu_slots_second, od_first, od_second)
    squares = squares + place.sibling(squares)
    for step in range(ring.bits):
        squares = squares + place.across(squares, step)
    grads_came = place.sibling(grads_sent)
    dy_step = after(dy_step, squares, grads_came)
    squares = jnp.sum(squares + vec_squares)
    dy_total = dy_keep[0].astype(F32) + dy_came[0].astype(F32) + dy_step.astype(F32)
    z_total = z_keep[0].astype(F32) + z_came[0].astype(F32) + z_step.astype(F32)
    start_grad = rows_backward(x_own, mid_grad, dy_total, gain_first)
    hidden_second = (hidden_first.astype(F32) + z_total + bias_second).astype(LOW)

    grad_norm = jnp.sqrt(squares)
    factor = jnp.minimum(1.0, CLIP_LEVEL / (grad_norm + 1e-06))

    def own_block(one, two):
        came = place.sibling(jnp.where(core == 0, two, one))
        mine = jnp.where(core == 0, one, two)
        return [jnp.where(core == h, mine, came) for h in range(2)]

    vec_share = after(vec, grads_sent).reshape(-1)[: ring.count * shard].reshape(ring.count, shard)
    vec_share = take(vec_share, lax.axis_index("dp"))[None]
    olds = (w_qkv, m_qkv, v_qkv, w_out, m_out, v_out, w_up, m_up, v_up, w_down, m_down, v_down)
    qus = (qu_slots_first, qu_slots_second)
    news = adam(info, factor[None], qus, (od_first, od_second), grads_came, olds)
    new_vec = adam_update(vectors, vec_share, m_vectors, v_vectors, factor, VECTOR_RATE)

    outputs = own_block(jnp.stack([hidden_first, start_grad]), jnp.stack([hidden_second, mid_grad]))
    outputs = jnp.concatenate(outputs, axis=1)
    hidden_out, input_grads = outputs[:1], outputs[1:]
    return (
        hidden_out,
        input_grads,
        *(news[3 * i] for i in range(4)),
        new_vec[0],
        *(news[3 * i + 1] for i in range(4)),
        new_vec[1],
        *(news[3 * i + 2] for i in range(4)),
        new_vec[2],
        grad_norm,
    )


def solution(mesh):
    return jax.shard_map(
        shards,
        mesh=mesh,
        in_specs=(
            P("dp", None),
            P("dp", None),
            P("dp", None),
            P("section", "dp", None),
            P("section", "dp", None),
            P("section", "dp", None),
            P("section", "dp", None),
            P("section", "dp"),
            P("section", "dp", None),
            P("section", "dp", None),
            P("section", "dp", None),
            P("section", "dp", None),
            P("section", "dp"),
            P("section", "dp", None),
            P("section", "dp", None),
            P("section", "dp", None),
            P("section", "dp", None),
            P("section", "dp"),
        ),
        out_specs=(
            P("section", "dp", None),
            P("section", "dp", None),
            P("section", "dp", None),
            P("section", "dp", None),
            P("section", "dp", None),
            P("section", "dp", None),
            P("section", "dp"),
            P("section", "dp", None),
            P("section", "dp", None),
            P("section", "dp", None),
            P("section", "dp", None),
            P("section", "dp"),
            P("section", "dp", None),
            P("section", "dp", None),
            P("section", "dp", None),
            P("section", "dp", None),
            P("section", "dp"),
            P(),
        ),
        check_vma=False,
    )
```

profile of v0, /device:TPU:1, one launch (start us, length us, event | category | flops | bytes accessed | tf_op | source)
XLA Modules:
  0.0 321.3 jit_solution(3600344714648818420)
XLA Ops:
  1.6 2.5 pack_weights.1
  6.8 2.3 collective-permute-start.5
  9.1 2.0 broadcast_select_fusion.1
  11.1 3.4 %collective-permute-start.3 = (bf16[64,1024]{1,0:T(8,128)(2,1)S(1)}, bf16[64,1024]{1,0:T(8,128)(2,1)S(1)}, u32[]{:S(2)}, u32[]{:S(2)}) collective-permute-start(bf16[64,1024]{1,0:T(8,128)(2,1)S(1)} %get-tuple-element.275), channel_id=1, source_target_pairs={{0,12},{1,13},{2,14},{3,15},{4,8},{5,9},{6,10},{7,11},{8,4},{9,5},... | collective-permute-start | bytes 393224 | tf_op jit(solution)/shard_map/ppermute | solution.py:87
  15.0 1.3 collective-permute-start.7
  16.2 1.3 collective-permute-done.3
  17.5 4.2 %collective-permute-done.1 = bf16[64,1024]{1,0:T(8,128)(2,1)S(1)} collective-permute-done((bf16[64,1024]{1,0:T(8,128)(2,1)S(1)}, bf16[64,1024]{1,0:T(8,128)(2,1)S(1)}, u32[]{:S(2)}, u32[]{:S(2)}) %collective-permute-start.1) | collective-permute-done | bytes 131104 | tf_op jit(solution)/shard_map/ppermute | solution.py:87
  21.8 3.4 %collective-permute-done.2 = bf16[64,1024]{1,0:T(8,128)(2,1)S(1)} collective-permute-done((bf16[64,1024]{1,0:T(8,128)(2,1)S(1)}, bf16[64,1024]{1,0:T(8,128)(2,1)S(1)}, u32[]{:S(2)}, u32[]{:S(2)}) %collective-permute-start.2) | collective-permute-done | bytes 131104 | tf_op jit(solution)/shard_map/ppermute | solution.py:87
  26.5 7.1 %collective-permute-done.6 = bf16[1,4,64,1024]{3,2,1,0:T(8,128)(2,1)S(1)} collective-permute-done((bf16[1,4,64,1024]{3,2,1,0:T(8,128)(2,1)S(1)}, bf16[1,4,64,1024]{3,2,1,0:T(8,128)(2,1)S(1)}, u32[]{:S(2)}, u32[]{:S(2)}) %collective-permute-start.6) | collective-permute-done | bytes 524320 | tf_op jit(solution)/shard_map/ppermute | solution.py:87
  33.7 2.3 collective-permute-start.9
  35.9 2.6 collective-permute-done.14.refs_10_
  38.6 4.9 %collective-permute-start.8 = (bf16[2,4,64,1024]{3,2,1,0:T(8,128)(2,1)S(1)}, bf16[2,4,64,1024]{3,2,1,0:T(8,128)(2,1)}, u32[]{:S(2)}, u32[]{:S(2)}) collective-permute-start(bf16[2,4,64,1024]{3,2,1,0:T(8,128)(2,1)S(1)} %constant_dynamic-update-slice_fusion.refs_0_), channel_id=1, source_target_pairs={{0,2},{1,3},{2,0},{3,1},{4,6},{5,7},{6,4},{7,5},{8,10},{9,11},{10,... | collective-permute-start | bytes 3145736 | tf_op jit(solution)/shard_map/ppermute | solution.py:87
  43.6 1.8 constant_dynamic-slice_fusion.1
  48.8 1.5 collective-permute-start.20
  50.7 1.8 collective-permute-start.22
  52.5 3.6 %collective-permute-done.8.refs_1_ = bf16[2,4,64,1024]{3,2,1,0:T(8,128)(2,1)} collective-permute-done((bf16[2,4,64,1024]{3,2,1,0:T(8,128)(2,1)S(1)}, bf16[2,4,64,1024]{3,2,1,0:T(8,128)(2,1)}, u32[]{:S(2)}, u32[]{:S(2)}) %collective-permute-start.8) | collective-permute-done | bytes 1048608 | tf_op jit(solution)/shard_map/ppermute | solution.py:87
  57.5 1.5 gather_fusion
  63.0 10.8 %forward_shard.1 = (bf16[128,1024]{1,0:T(8,128)(2,1)S(1)}, bf16[128,1024]{1,0:T(8,128)(2,1)S(1)}, bf16[128,1024]{1,0:T(8,128)(2,1)S(1)}, bf16[128,1024]{1,0:T(8,...) custom-call(s32[3]{0:T(128)S(1)} %pad_add_fusion.info, ...), custom_call_target="tpu_custom_call" | custom-call | flops 6442450944 | bytes 33554432 | tf_op jit(solution)/shard_map/forward_shard/pallas_call | solution.py:521
  73.9 1.6 collective-permute-start.17
  75.5 1.5 collective-permute-start.16
  77.6 1.3 collective-permute-done.21.refs_14_
  81.3 22.7 %collective-permute-done.18 = bf16[128,1024]{1,0:T(8,128)(2,1)S(1)} collective-permute-done((bf16[128,1024]{1,0:T(8,128)(2,1)S(1)}, bf16[128,1024]{1,0:T(8,128)(2,1)S(1)}, u32[]{:S(2)}, u32[]{:S(2)}) %collective-permute-start.18) | collective-permute-done | bytes 262176 | tf_op jit(solution)/shard_map/ppermute | solution.py:87
  104.6 2.4 collective-permute-start.24
  107.0 5.8 %collective-permute-start.25 = (bf16[128,1024]{1,0:T(8,128)(2,1)S(1)}, bf16[128,1024]{1,0:T(8,128)(2,1)S(1)}, u32[]{:S(2)}, u32[]{:S(2)}) collective-permute-start(bf16[128,1024]{1,0:T(8,128)(2,1)S(1)} %get-tuple-element.261.refs_8_), channel_id=1, source_target_pairs={{0,4},{1,5},{2,6},{3,7},{4,0},{5,1},{6,2},{7,3},{8,12},{9,13},{10,... | collective-permute-start | bytes 786440 | tf_op jit(solution)/shard_map/ppermute | solution.py:87
  113.2 1.7 collective-permute-start.27
  115.1 4.3 %collective-permute-done.25.refs_9_ = bf16[128,1024]{1,0:T(8,128)(2,1)S(1)} collective-permute-done((bf16[128,1024]{1,0:T(8,128)(2,1)S(1)}, bf16[128,1024]{1,0:T(8,128)(2,1)S(1)}, u32[]{:S(2)}, u32[]{:S(2)}) %collective-permute-start.25) | collective-permute-done | bytes 262176 | tf_op jit(solution)/shard_map/ppermute | solution.py:87
  119.4 1.9 collective-permute-done.26.refs_10_
  121.3 7.7 %collective-permute-done.27.refs_11_ = bf16[128,1024]{1,0:T(8,128)(2,1)S(1)} collective-permute-done((bf16[128,1024]{1,0:T(8,128)(2,1)S(1)}, bf16[128,1024]{1,0:T(8,128)(2,1)S(1)}, u32[]{:S(2)}, u32[]{:S(2)}) %collective-permute-start.27) | collective-permute-done | bytes 262176 | tf_op jit(solution)/shard_map/ppermute | solution.py:87
  129.0 7.3 %collective-permute-start.29 = (bf16[2,4,64,1024]{3,2,1,0:T(8,128)(2,1)S(1)}, bf16[2,4,64,1024]{3,2,1,0:T(8,128)(2,1)S(1)}, u32[]{:S(2)}, u32[]{:S(2)}) collective-permute-start(bf16[2,4,64,1024]{3,2,1,0:T(8,128)(2,1)S(1)} %pad_maximum_fusion.refs_0_), channel_id=1, source_target_pairs={{0,16},{1,17},{2,18},{3,19},{4,20},{5,21},{6,22},{7,23},{8,24},{9,... | collective-permute-start | bytes 3145736 | tf_op jit(solution)/shard_map/ppermute | solution.py:87
  136.9 4.1 %collective-permute-done.31.refs_6_ = bf16[2,320,512]{2,1,0:T(8,128)(2,1)S(1)} collective-permute-done((bf16[2,320,512]{2,1,0:T(8,128)(2,1)S(1)}, bf16[2,320,512]{2,1,0:T(8,128)(2,1)S(1)}, u32[]{:S(2)}, u32[]{:S(2)}) %collective-permute-start.31) | collective-permute-done | bytes 655392 | tf_op jit(solution)/shard_map/ppermute | solution.py:87
  142.0 13.3 %forward_backward_shard.1 = (bf16[128,1024]{1,0:T(8,128)(2,1)S(1)}, bf16[128,1024]{1,0:T(8,128)(2,1)S(1)}, bf16[128,1024]{1,0:T(8,128)(2,1)S(1)}, bf16[128,1024]...) custom-call(s32[3]{0:T(128)S(1)} %pad_add_fusion.info, ...), custom_call_target="tpu_custom_call" | custom-call | flops 12884901888 | bytes 33554432 | tf_op jit(solution)/shard_map/forward_backward_shard/pallas_call | solution.py:583
  155.3 3.4 %collective-permute-start.33 = (bf16[128,1024]{1,0:T(8,128)(2,1)S(1)}, bf16[128,1024]{1,0:T(8,128)(2,1)S(1)}, u32[]{:S(2)}, u32[]{:S(2)}) collective-permute-start(bf16[128,1024]{1,0:T(8,128)(2,1)S(1)} %get-tuple-element.169), channel_id=1, source_target_pairs={{0,4},{1,5},{2,6},{3,7},{4,0},{5,1},{6,2},{7,3},{8,12},{9,13},{10,... | collective-permute-start | bytes 786440 | tf_op jit(solution)/shard_map/ppermute | solution.py:87
  159.1 1.7 collective-permute-start.35
  160.9 6.4 %weight_grads.1 = (bf16[12400,128]{1,0:T(8,128)(2,1)S(1)}, bf16[12400,128]{1,0:T(8,128)(2,1)S(1)}) custom-call(s32[3]{0:T(128)S(1)} %pad_add_fusion.info, bf16[512,256]{1,0:T(8,128)(2,1)} %get-tuple-element.172.far_mixed, bf16[512,1024]{1,0:T(8,128)(2,1)} %get-tuple-element.173.far_active, bf16[512,1024]{1,0:T(8,128)(2,1)} %get-tuple-element.174.far_grad, ...), custom_call_target="tpu_custom_call" | custom-call | flops 99999997952 | bytes 25165824 | tf_op jit(solution)/shard_map/weight_grads/pallas_call | solution.py:742
  167.3 2.5 collective-permute-done.33
  169.8 7.8 %collective-permute-done.35 = bf16[128,1024]{1,0:T(8,128)(2,1)S(1)} collective-permute-done((bf16[128,1024]{1,0:T(8,128)(2,1)S(1)}, bf16[128,1024]{1,0:T(8,128)(2,1)S(1)}, u32[]{:S(2)}, u32[]{:S(2)}) %collective-permute-start.35) | collective-permute-done | bytes 262176 | tf_op jit(solution)/shard_map/ppermute | solution.py:87
  177.6 3.1 collective-permute-start.36
  181.6 4.5 %collective-permute-done.36.came = bf16[12400,128]{1,0:T(8,128)(2,1)S(1)} collective-permute-done((bf16[12400,128]{1,0:T(8,128)(2,1)S(1)}, bf16[12400,128]{1,0:T(8,128)(2,1)S(1)}, u32[]{:S(2)}, u32[]{:S(2)}) %collective-permute-start.36) | collective-permute-done | bytes 3174432 | tf_op jit(solution)/shard_map/ppermute | solution.py:87
  187.0 4.8 %collective-permute-start.38 = (bf16[128,1024]{1,0:T(8,128)(2,1)S(1)}, bf16[128,1024]{1,0:T(8,128)(2,1)S(1)}, u32[]{:S(2)}, u32[]{:S(2)}) collective-permute-start(bf16[128,1024]{1,0:T(8,128)(2,1)S(1)} %fusion.18.refs_0_), channel_id=1, source_target_pairs={{0,4},{1,5},{2,6},{3,7},{4,0},{5,1},{6,2},{7,3},{8,12},{9,13},{10,... | collective-permute-start | bytes 786440 | tf_op jit(solution)/shard_map/ppermute | solution.py:87
  192.2 1.7 collective-permute-start.40
  194.0 5.1 %collective-permute-done.38.refs_1_ = bf16[128,1024]{1,0:T(8,128)(2,1)S(1)} collective-permute-done((bf16[128,1024]{1,0:T(8,128)(2,1)S(1)}, bf16[128,1024]{1,0:T(8,128)(2,1)S(1)}, u32[]{:S(2)}, u32[]{:S(2)}) %collective-permute-start.38) | collective-permute-done | bytes 262176 | tf_op jit(solution)/shard_map/ppermute | solution.py:87
  199.1 1.7 collective-permute-done.39.refs_2_
  200.8 8.1 %collective-permute-done.40.refs_3_ = bf16[128,1024]{1,0:T(8,128)(2,1)S(1)} collective-permute-done((bf16[128,1024]{1,0:T(8,128)(2,1)S(1)}, bf16[128,1024]{1,0:T(8,128)(2,1)S(1)}, u32[]{:S(2)}, u32[]{:S(2)}) %collective-permute-start.40) | collective-permute-done | bytes 262176 | tf_op jit(solution)/shard_map/ppermute | solution.py:87
  208.9 7.1 %collective-permute-start.46 = (bf16[2,128,1024]{2,1,0:T(8,128)(2,1)S(1)}, bf16[2,128,1024]{2,1,0:T(8,128)(2,1)S(1)}, u32[]{:S(2)}, u32[]{:S(2)}) collective-permute-start(bf16[2,128,1024]{2,1,0:T(8,128)(2,1)S(1)} %copy-done.15), channel_id=1, source_target_pairs={{0,4},{1,5},{2,6},{3,7},{4,0},{5,1},{6,2},{7,3},{8,12},{9,13},{10,... | collective-permute-start | bytes 1572872 | tf_op jit(solution)/shard_map/ppermute | solution.py:87
  216.4 2.9 collective-permute-start.41
  219.3 12.4 %backward_shard.1 = (bf16[2,128,1024]{2,1,0:T(8,128)(2,1)S(1)}, bf16[2,128,1024]{2,1,0:T(8,128)(2,1)S(1)}, bf16[12400,128]{1,0:T(8,128)(2,1)S(1)}, bf16[12400,128]{1,0:T(8,128)(2,1)S(1)}) custom-call(s32[3]{0:T(128)S(1)} %pad_add_fusion.info, bf16[128,1024]{1,0:T(8,128)(2,1)S(1)} %fusion.18.refs_0_, bf16[128,1024]{1,0:T(8,128)(2,1)S(1)} %collective-permute-done.38.refs_1_, ...), custom_call_target="tpu_custom_call" | custom-call | flops 12884901888 | bytes 33554432 | tf_op jit(solution)/shard_map/backward_shard/pallas_call | solution.py:637
  232.0 1.8 collective-permute-start.47
  233.8 5.3 %collective-permute-done.47.came = bf16[12400,128]{1,0:T(8,128)(2,1)S(1)} collective-permute-done((bf16[12400,128]{1,0:T(8,128)(2,1)S(1)}, bf16[12400,128]{1,0:T(8,128)(2,1)S(1)}, u32[]{:S(2)}, u32[]{:S(2)}) %collective-permute-start.47) | collective-permute-done | bytes 3174432 | tf_op jit(solution)/shard_map/ppermute | solution.py:87
  239.8 1.3 collective-permute-start.48
  241.2 1.5 collective-permute-start.42
  243.2 1.7 collective-permute-start.44
  244.9 14.9 %collective-permute-done.48.came = bf16[6256,128]{1,0:T(8,128)(2,1)S(1)} collective-permute-done((bf16[6256,128]{1,0:T(8,128)(2,1)S(1)}, bf16[6256,128]{1,0:T(8,128)(2,1)S(1)}, u32[]{:S(2)}, u32[]{:S(2)}) %collective-permute-start.48) | collective-permute-done | bytes 1601568 | tf_op jit(solution)/shard_map/ppermute | solution.py:87
  260.2 1.4 collective-permute-start.50
  261.9 14.0 %collective-permute-done.45 = bf16[2,128,1024]{2,1,0:T(8,128)(2,1)S(1)} collective-permute-done((bf16[2,128,1024]{2,1,0:T(8,128)(2,1)S(1)}, bf16[2,128,1024]{2,1,0:T(8,128)(2,1)S(1)}, u32[]{:S(2)}, u32[]{:S(2)}) %collective-permute-start.45) | collective-permute-done | bytes 524320 | tf_op jit(solution)/shard_map/ppermute | solution.py:87
  277.0 1.8 collective-permute-start.52
  278.8 1.7 collective-permute-start.53
  280.5 2.2 collective-permute-done.51.refs_1_
  282.7 4.6 %collective-permute-done.53.refs_3_ = bf16[560,128]{1,0:T(8,128)(2,1)S(1)} collective-permute-done((bf16[560,128]{1,0:T(8,128)(2,1)S(1)}, bf16[560,128]{1,0:T(8,128)(2,1)S(1)}, u32[]{:S(2)}, u32[]{:S(2)}) %collective-permute-start.53) | collective-permute-done | bytes 143392 | tf_op jit(solution)/shard_map/ppermute | solution.py:87
  288.0 4.5 %collective-permute-start.55 = (f32[8,128]{1,0:T(8,128)S(1)}, f32[8,128]{1,0:T(8,128)S(1)}, u32[]{:S(2)}, u32[]{:S(2)}) collective-permute-start(f32[8,128]{1,0:T(8,128)S(1)} %get-tuple-element.226), channel_id=1, source_target_pairs={{0,16},{1,17},{2,18},{3,19},{4,20},{5,21},{6,22},{7,23},{8,24},{9,... | collective-permute-start | bytes 12296 | tf_op jit(solution)/shard_map/ppermute | solution.py:87
  293.8 1.9 collective-permute-start.54
  297.0 1.2 collective-permute-done.57
  298.8 3.3 %collective-permute-done.54 = bf16[128,1024]{1,0:T(8,128)(2,1)S(1)} collective-permute-done((bf16[128,1024]{1,0:T(8,128)(2,1)S(1)}, bf16[128,1024]{1,0:T(8,128)(2,1)S(1)}, u32[]{:S(2)}, u32[]{:S(2)}) %collective-permute-start.54) | collective-permute-done | bytes 262176 | tf_op jit(solution)/shard_map/ppermute | solution.py:87
  304.4 2.7 collective-permute-start.59
  308.6 8.9 %adamw.1 = (f32[1,64,3072]{2,1,0:T(8,128)}, f32[1,64,3072]{2,1,0:T(8,128)}, f32[1,64,3072]{2,1,0:T(8,128)}, f32[1,64,1024]{2,1,0:T(8,128)}, f32[1,64,1024]{2,1,0...) custom-call(s32[3]{0:T(128)S(1)} %pad_add_fusion.info, ...), custom_call_target="tpu_custom_call" | custom-call | tf_op jit(solution)/shard_map/adamw/pallas_call | solution.py:933
  (195 shorter events, 35.7 us)
Async XLA Ops:
  4.1 1.9 collective-permute-start.4
  4.2 4.9 %collective-permute-start = (bf16[4,64,1024]{2,1,0:T(8,128)(2,1)S(1)}, bf16[4,64,1024]{2,1,0:T(8,128)(2,1)}, u32[]{:S(2)}, u32[]{:S(2)}) collective-permute-start(bf16[4,64,1024]{2,1,0:T(8,128)(2,1)S(1)} %get-tuple-element.138), channel_id=1, source_target_pairs={{0,16},{1,17},{2,18},{3,19},{4,20},{5,21},{6,22},{7,23},{8,24},{9,... | collective-permute-start | bytes 1572872 | tf_op jit(solution)/shard_map/ppermute | solution.py:87
  5.8 39.6 %copy-start.7 = (bf16[128,1024]{1,0:T(8,128)(2,1)}, bf16[128,1024]{1,0:T(8,128)(2,1)S(1)}, u32[]{:S(2)}) copy-start(bf16[128,1024]{1,0:T(8,128)(2,1)S(1)} %dynamic-slice_bitcast_fusion.refs_12_) | copy-start | bytes 786436
  6.8 8.1 %collective-permute-start.5 = (bf16[1,320,512]{2,1,0:T(8,128)(2,1)S(1)}, bf16[1,320,512]{2,1,0:T(8,128)(2,1)S(1)}, u32[]{:S(2)}, u32[]{:S(2)}) collective-permute-start(bf16[1,320,512]{2,1,0:T(8,128)(2,1)S(1)} %get-tuple-element.269), channel_id=1, source_target_pairs={{0,1},{1,0},{2,3},{3,2},{4,5},{5,4},{6,7},{7,6},{8,9},{9,8},{10,11... | collective-permute-start | bytes 983048 | tf_op jit(solution)/shard_map/ppermute | solution.py:87
  11.1 6.4 %collective-permute-start.3 = (bf16[64,1024]{1,0:T(8,128)(2,1)S(1)}, bf16[64,1024]{1,0:T(8,128)(2,1)S(1)}, u32[]{:S(2)}, u32[]{:S(2)}) collective-permute-start(bf16[64,1024]{1,0:T(8,128)(2,1)S(1)} %get-tuple-element.275), channel_id=1, source_target_pairs={{0,12},{1,13},{2,14},{3,15},{4,8},{5,9},{6,10},{7,11},{8,4},{9,5},... | collective-permute-start | bytes 393224 | tf_op jit(solution)/shard_map/ppermute | solution.py:87
  14.5 7.3 %collective-permute-start.1 = (bf16[64,1024]{1,0:T(8,128)(2,1)S(1)}, bf16[64,1024]{1,0:T(8,128)(2,1)S(1)}, u32[]{:S(2)}, u32[]{:S(2)}) collective-permute-start(bf16[64,1024]{1,0:T(8,128)(2,1)S(1)} %get-tuple-element.277), channel_id=1, source_target_pairs={{0,4},{1,5},{2,6},{3,7},{4,0},{5,1},{6,2},{7,3},{8,12},{9,13},{10,... | collective-permute-start | bytes 393224 | tf_op jit(solution)/shard_map/ppermute | solution.py:87
  14.5 10.7 %collective-permute-start.2 = (bf16[64,1024]{1,0:T(8,128)(2,1)S(1)}, bf16[64,1024]{1,0:T(8,128)(2,1)S(1)}, u32[]{:S(2)}, u32[]{:S(2)}) collective-permute-start(bf16[64,1024]{1,0:T(8,128)(2,1)S(1)} %get-tuple-element.276), channel_id=1, source_target_pairs={{0,8},{1,9},{2,10},{3,11},{4,12},{5,13},{6,14},{7,15},{8,0},{9,1},... | collective-permute-start | bytes 393224 | tf_op jit(solution)/shard_map/ppermute | solution.py:87
  15.0 23.6 %collective-permute-start.7 = (bf16[2,320,512]{2,1,0:T(8,128)(2,1)S(1)}, bf16[2,320,512]{2,1,0:T(8,128)(2,1)}, u32[]{:S(2)}, u32[]{:S(2)}) collective-permute-start(bf16[2,320,512]{2,1,0:T(8,128)(2,1)S(1)} %pad_maximum_fusion.1.refs_2_), channel_id=1, source_target_pairs={{0,2},{1,3},{2,0},{3,1},{4,6},{5,7},{6,4},{7,5},{8,10},{9,11},{10,... | collective-permute-start | bytes 1966088 | tf_op jit(solution)/shard_map/ppermute | solution.py:87
  25.2 8.4 %collective-permute-start.6 = (bf16[1,4,64,1024]{3,2,1,0:T(8,128)(2,1)S(1)}, bf16[1,4,64,1024]{3,2,1,0:T(8,128)(2,1)S(1)}, u32[]{:S(2)}, u32[]{:S(2)}) collective-permute-start(bf16[1,4,64,1024]{3,2,1,0:T(8,128)(2,1)S(1)} %maximum_bitcast_fusion), channel_id=1, source_target_pairs={{0,1},{1,0},{2,3},{3,2},{4,5},{5,4},{6,7},{7,6},{8,9},{9,8},{10,11... | collective-permute-start | bytes 1572872 | tf_op jit(solution)/shard_map/ppermute | solution.py:87
  25.5 13.1 %collective-permute-start.14 = (bf16[144,1024]{1,0:T(8,128)(2,1)S(1)}, bf16[144,1024]{1,0:T(8,128)(2,1)S(1)}, u32[]{:S(2)}, u32[]{:S(2)}) collective-permute-start(bf16[144,1024]{1,0:T(8,128)(2,1)S(1)} %fusion.27.refs_8_), channel_id=1, source_target_pairs={{0,8},{1,9},{2,10},{3,11},{4,12},{5,13},{6,14},{7,15},{8,0},{9,1},... | collective-permute-start | bytes 884744 | tf_op jit(solution)/shard_map/ppermute | solution.py:87
  25.7 20.8 %collective-permute-start.13 = (bf16[144,1024]{1,0:T(8,128)(2,1)S(1)}, bf16[144,1024]{1,0:T(8,128)(2,1)S(1)}, u32[]{:S(2)}, u32[]{:S(2)}) collective-permute-start(bf16[144,1024]{1,0:T(8,128)(2,1)S(1)} %fusion.27.refs_8_), channel_id=1, source_target_pairs={{0,4},{1,5},{2,6},{3,7},{4,0},{5,1},{6,2},{7,3},{8,12},{9,13},{10,... | collective-permute-start | bytes 884744 | tf_op jit(solution)/shard_map/ppermute | solution.py:87
  33.7 15.1 %collective-permute-start.9 = (bf16[2,4,64,1024]{3,2,1,0:T(8,128)(2,1)S(1)}, bf16[2,4,64,1024]{3,2,1,0:T(8,128)(2,1)}, u32[]{:S(2)}, u32[]{:S(2)}) collective-permute-start(bf16[2,4,64,1024]{3,2,1,0:T(8,128)(2,1)S(1)} %constant_dynamic-update-slice_fusion.refs_0_), channel_id=1, source_target_pairs={{0,16},{1,17},{2,18},{3,19},{4,20},{5,21},{6,22},{7,23},{8,24},{9,... | collective-permute-start | bytes 3145736 | tf_op jit(solution)/shard_map/ppermute | solution.py:87
  38.6 8.5 %collective-permute-start.15 = (bf16[144,1024]{1,0:T(8,128)(2,1)S(1)}, bf16[144,1024]{1,0:T(8,128)(2,1)S(1)}, u32[]{:S(2)}, u32[]{:S(2)}) collective-permute-start(bf16[144,1024]{1,0:T(8,128)(2,1)S(1)} %collective-permute-done.14.refs_10_), channel_id=1, source_target_pairs={{0,4},{1,5},{2,6},{3,7},{4,0},{5,1},{6,2},{7,3},{8,12},{9,13},{10,... | collective-permute-start | bytes 884744 | tf_op jit(solution)/shard_map/ppermute | solution.py:87
  38.6 17.5 %collective-permute-start.8 = (bf16[2,4,64,1024]{3,2,1,0:T(8,128)(2,1)S(1)}, bf16[2,4,64,1024]{3,2,1,0:T(8,128)(2,1)}, u32[]{:S(2)}, u32[]{:S(2)}) collective-permute-start(bf16[2,4,64,1024]{3,2,1,0:T(8,128)(2,1)S(1)} %constant_dynamic-update-slice_fusion.refs_0_), channel_id=1, source_target_pairs={{0,2},{1,3},{2,0},{3,1},{4,6},{5,7},{6,4},{7,5},{8,10},{9,11},{10,... | collective-permute-start | bytes 3145736 | tf_op jit(solution)/shard_map/ppermute | solution.py:87
  46.5 2.3 collective-permute-start.11
  46.5 15.5 %collective-permute-start.12 = (bf16[2,320,512]{2,1,0:T(8,128)(2,1)}, bf16[2,320,512]{2,1,0:T(8,128)(2,1)}, u32[]{:S(2)}, u32[]{:S(2)}) collective-permute-start(bf16[2,320,512]{2,1,0:T(8,128)(2,1)} %collective-permute-done.7.refs_3_), channel_id=1, source_target_pairs={{0,16},{1,17},{2,18},{3,19},{4,20},{5,21},{6,22},{7,23},{8,24},{9,... | collective-permute-start | bytes 1966088 | tf_op jit(solution)/shard_map/ppermute | solution.py:87
  48.8 28.1 %collective-permute-start.20 = (bf16[192,1024]{1,0:T(8,128)(2,1)}, bf16[192,1024]{1,0:T(8,128)(2,1)}, u32[]{:S(2)}, u32[]{:S(2)}) collective-permute-start(bf16[192,1024]{1,0:T(8,128)(2,1)} %get-tuple-element.152), channel_id=1, source_target_pairs={{0,4},{1,5},{2,6},{3,7},{4,0},{5,1},{6,2},{7,3},{8,12},{9,13},{10,... | collective-permute-start | bytes 1179656 | tf_op jit(solution)/shard_map/ppermute | solution.py:87
  50.3 28.5 %collective-permute-start.21 = (bf16[192,1024]{1,0:T(8,128)(2,1)}, bf16[192,1024]{1,0:T(8,128)(2,1)}, u32[]{:S(2)}, u32[]{:S(2)}) collective-permute-start(bf16[192,1024]{1,0:T(8,128)(2,1)} %get-tuple-element.154), channel_id=1, source_target_pairs={{0,8},{1,9},{2,10},{3,11},{4,12},{5,13},{6,14},{7,15},{8,0},{9,1},... | collective-permute-start | bytes 1179656 | tf_op jit(solution)/shard_map/ppermute | solution.py:87
  50.7 29.2 %collective-permute-start.22 = (bf16[192,1024]{1,0:T(8,128)(2,1)}, bf16[192,1024]{1,0:T(8,128)(2,1)}, u32[]{:S(2)}, u32[]{:S(2)}) collective-permute-start(bf16[192,1024]{1,0:T(8,128)(2,1)} %get-tuple-element.156), channel_id=1, source_target_pairs={{0,12},{1,13},{2,14},{3,15},{4,8},{5,9},{6,10},{7,11},{8,4},{9,5},... | collective-permute-start | bytes 1179656 | tf_op jit(solution)/shard_map/ppermute | solution.py:87
  56.1 6.0 %collective-permute-start.10 = (bf16[2,4,64,1024]{3,2,1,0:T(8,128)(2,1)}, bf16[2,4,64,1024]{3,2,1,0:T(8,128)(2,1)}, u32[]{:S(2)}, u32[]{:S(2)}) collective-permute-start(bf16[2,4,64,1024]{3,2,1,0:T(8,128)(2,1)} %collective-permute-done.8.refs_1_), channel_id=1, source_target_pairs={{0,16},{1,17},{2,18},{3,19},{4,20},{5,21},{6,22},{7,23},{8,24},{9,... | collective-permute-start | bytes 3145736 | tf_op jit(solution)/shard_map/ppermute | solution.py:87
  63.0 17.9 %copy-start.11 = (bf16[1,64,1024]{2,1,0:T(8,128)(2,1)S(1)}, bf16[1,64,1024]{2,1,0:T(8,128)(2,1)}, u32[]{:S(2)}) copy-start(bf16[1,64,1024]{2,1,0:T(8,128)(2,1)} %get-tuple-element.270) | copy-start | bytes 393220
  73.9 30.2 %copy-start.3 = (bf16[128,1024]{1,0:T(8,128)(2,1)S(1)}, bf16[128,1024]{1,0:T(8,128)(2,1)}, u32[]{:S(2)}) copy-start(bf16[128,1024]{1,0:T(8,128)(2,1)} %copy-done.2) | copy-start | bytes 786436
  73.9 30.1 %collective-permute-start.17 = (bf16[1,320,512]{2,1,0:T(8,128)(2,1)S(1)}, bf16[1,320,512]{2,1,0:T(8,128)(2,1)S(1)}, u32[]{:S(2)}, u32[]{:S(2)}) collective-permute-start(bf16[1,320,512]{2,1,0:T(8,128)(2,1)S(1)} %copy-done.6), channel_id=1, source_target_pairs={{0,1},{1,0},{2,3},{3,2},{4,5},{5,4},{6,7},{7,6},{8,9},{9,8},{10,11... | collective-permute-start | bytes 983048 | tf_op jit(solution)/shard_map/ppermute | solution.py:87
  75.5 28.6 %collective-permute-start.16 = (bf16[128,1024]{1,0:T(8,128)(2,1)S(1)}, bf16[128,1024]{1,0:T(8,128)(2,1)S(1)}, u32[]{:S(2)}, u32[]{:S(2)}) collective-permute-start(bf16[128,1024]{1,0:T(8,128)(2,1)S(1)} %get-tuple-element.146), channel_id=1, source_target_pairs={{0,4},{1,5},{2,6},{3,7},{4,0},{5,1},{6,2},{7,3},{8,12},{9,13},{10,... | collective-permute-start | bytes 786440 | tf_op jit(solution)/shard_map/ppermute | solution.py:87
  76.9 27.1 %collective-permute-start.18 = (bf16[128,1024]{1,0:T(8,128)(2,1)S(1)}, bf16[128,1024]{1,0:T(8,128)(2,1)S(1)}, u32[]{:S(2)}, u32[]{:S(2)}) collective-permute-start(bf16[128,1024]{1,0:T(8,128)(2,1)S(1)} %get-tuple-element.149), channel_id=1, source_target_pairs={{0,8},{1,9},{2,10},{3,11},{4,12},{5,13},{6,14},{7,15},{8,0},{9,1},... | collective-permute-start | bytes 786440 | tf_op jit(solution)/shard_map/ppermute | solution.py:87
  78.9 25.2 %collective-permute-start.19 = (bf16[128,1024]{1,0:T(8,128)(2,1)S(1)}, bf16[128,1024]{1,0:T(8,128)(2,1)S(1)}, u32[]{:S(2)}, u32[]{:S(2)}) collective-permute-start(bf16[128,1024]{1,0:T(8,128)(2,1)S(1)} %get-tuple-element.151), channel_id=1, source_target_pairs={{0,12},{1,13},{2,14},{3,15},{4,8},{5,9},{6,10},{7,11},{8,4},{9,5},... | collective-permute-start | bytes 786440 | tf_op jit(solution)/shard_map/ppermute | solution.py:87
  81.0 23.4 %collective-permute-start.23 = (bf16[1,4,64,1024]{3,2,1,0:T(8,128)(2,1)S(1)}, bf16[1,4,64,1024]{3,2,1,0:T(8,128)(2,1)S(1)}, u32[]{:S(2)}, u32[]{:S(2)}) collective-permute-start(bf16[1,4,64,1024]{3,2,1,0:T(8,128)(2,1)S(1)} %maximum_bitcast_fusion.1), channel_id=1, source_target_pairs={{0,1},{1,0},{2,3},{3,2},{4,5},{5,4},{6,7},{7,6},{8,9},{9,8},{10,11... | collective-permute-start | bytes 1572872 | tf_op jit(solution)/shard_map/ppermute | solution.py:87
  104.6 31.7 %collective-permute-start.24 = (bf16[2,4,64,1024]{3,2,1,0:T(8,128)(2,1)S(1)}, bf16[2,4,64,1024]{3,2,1,0:T(8,128)(2,1)S(1)}, u32[]{:S(2)}, u32[]{:S(2)}) collective-permute-start(bf16[2,4,64,1024]{3,2,1,0:T(8,128)(2,1)S(1)} %pad_maximum_fusion.refs_0_), channel_id=1, source_target_pairs={{0,2},{1,3},{2,0},{3,1},{4,6},{5,7},{6,4},{7,5},{8,10},{9,11},{10,... | collective-permute-start | bytes 3145736 | tf_op jit(solution)/shard_map/ppermute | solution.py:87
  107.0 12.4 %collective-permute-start.25 = (bf16[128,1024]{1,0:T(8,128)(2,1)S(1)}, bf16[128,1024]{1,0:T(8,128)(2,1)S(1)}, u32[]{:S(2)}, u32[]{:S(2)}) collective-permute-start(bf16[128,1024]{1,0:T(8,128)(2,1)S(1)} %get-tuple-element.261.refs_8_), channel_id=1, source_target_pairs={{0,4},{1,5},{2,6},{3,7},{4,0},{5,1},{6,2},{7,3},{8,12},{9,13},{10,... | collective-permute-start | bytes 786440 | tf_op jit(solution)/shard_map/ppermute | solution.py:87
  112.8 8.5 %collective-permute-start.26 = (bf16[128,1024]{1,0:T(8,128)(2,1)S(1)}, bf16[128,1024]{1,0:T(8,128)(2,1)S(1)}, u32[]{:S(2)}, u32[]{:S(2)}) collective-permute-start(bf16[128,1024]{1,0:T(8,128)(2,1)S(1)} %get-tuple-element.261.refs_8_), channel_id=1, source_target_pairs={{0,8},{1,9},{2,10},{3,11},{4,12},{5,13},{6,14},{7,15},{8,0},{9,1},... | collective-permute-start | bytes 786440 | tf_op jit(solution)/shard_map/ppermute | solution.py:87
  113.2 15.8 %collective-permute-start.27 = (bf16[128,1024]{1,0:T(8,128)(2,1)S(1)}, bf16[128,1024]{1,0:T(8,128)(2,1)S(1)}, u32[]{:S(2)}, u32[]{:S(2)}) collective-permute-start(bf16[128,1024]{1,0:T(8,128)(2,1)S(1)} %get-tuple-element.261.refs_8_), channel_id=1, source_target_pairs={{0,12},{1,13},{2,14},{3,15},{4,8},{5,9},{6,10},{7,11},{8,4},{9,5},... | collective-permute-start | bytes 786440 | tf_op jit(solution)/shard_map/ppermute | solution.py:87
  114.9 21.9 %collective-permute-start.28 = (bf16[2,320,512]{2,1,0:T(8,128)(2,1)S(1)}, bf16[2,320,512]{2,1,0:T(8,128)(2,1)S(1)}, u32[]{:S(2)}, u32[]{:S(2)}) collective-permute-start(bf16[2,320,512]{2,1,0:T(8,128)(2,1)S(1)} %constant_dynamic-update-slice_fusion.2.refs_2_), channel_id=1, source_target_pairs={{0,2},{1,3},{2,0},{3,1},{4,6},{5,7},{6,4},{7,5},{8,10},{9,11},{10,... | collective-permute-start | bytes 1966088 | tf_op jit(solution)/shard_map/ppermute | solution.py:87
  129.0 13.0 %collective-permute-start.29 = (bf16[2,4,64,1024]{3,2,1,0:T(8,128)(2,1)S(1)}, bf16[2,4,64,1024]{3,2,1,0:T(8,128)(2,1)S(1)}, u32[]{:S(2)}, u32[]{:S(2)}) collective-permute-start(bf16[2,4,64,1024]{3,2,1,0:T(8,128)(2,1)S(1)} %pad_maximum_fusion.refs_0_), channel_id=1, source_target_pairs={{0,16},{1,17},{2,18},{3,19},{4,20},{5,21},{6,22},{7,23},{8,24},{9,... | collective-permute-start | bytes 3145736 | tf_op jit(solution)/shard_map/ppermute | solution.py:87
  136.3 5.7 %collective-permute-start.30 = (bf16[2,4,64,1024]{3,2,1,0:T(8,128)(2,1)S(1)}, bf16[2,4,64,1024]{3,2,1,0:T(8,128)(2,1)S(1)}, u32[]{:S(2)}, u32[]{:S(2)}) collective-permute-start(bf16[2,4,64,1024]{3,2,1,0:T(8,128)(2,1)S(1)} %collective-permute-done.24.refs_1_), channel_id=1, source_target_pairs={{0,16},{1,17},{2,18},{3,19},{4,20},{5,21},{6,22},{7,23},{8,24},{9,... | collective-permute-start | bytes 3145736 | tf_op jit(solution)/shard_map/ppermute | solution.py:87
  136.4 4.7 %collective-permute-start.31 = (bf16[2,320,512]{2,1,0:T(8,128)(2,1)S(1)}, bf16[2,320,512]{2,1,0:T(8,128)(2,1)S(1)}, u32[]{:S(2)}, u32[]{:S(2)}) collective-permute-start(bf16[2,320,512]{2,1,0:T(8,128)(2,1)S(1)} %constant_dynamic-update-slice_fusion.2.refs_2_), channel_id=1, source_target_pairs={{0,16},{1,17},{2,18},{3,19},{4,20},{5,21},{6,22},{7,23},{8,24},{9,... | collective-permute-start | bytes 1966088 | tf_op jit(solution)/shard_map/ppermute | solution.py:87
  136.8 5.1 %collective-permute-start.32 = (bf16[2,320,512]{2,1,0:T(8,128)(2,1)S(1)}, bf16[2,320,512]{2,1,0:T(8,128)(2,1)S(1)}, u32[]{:S(2)}, u32[]{:S(2)}) collective-permute-start(bf16[2,320,512]{2,1,0:T(8,128)(2,1)S(1)} %collective-permute-done.28.refs_3_), channel_id=1, source_target_pairs={{0,16},{1,17},{2,18},{3,19},{4,20},{5,21},{6,22},{7,23},{8,24},{9,... | collective-permute-start | bytes 1966088 | tf_op jit(solution)/shard_map/ppermute | solution.py:87
  155.3 14.5 %collective-permute-start.33 = (bf16[128,1024]{1,0:T(8,128)(2,1)S(1)}, bf16[128,1024]{1,0:T(8,128)(2,1)S(1)}, u32[]{:S(2)}, u32[]{:S(2)}) collective-permute-start(bf16[128,1024]{1,0:T(8,128)(2,1)S(1)} %get-tuple-element.169), channel_id=1, source_target_pairs={{0,4},{1,5},{2,6},{3,7},{4,0},{5,1},{6,2},{7,3},{8,12},{9,13},{10,... | collective-permute-start | bytes 786440 | tf_op jit(solution)/shard_map/ppermute | solution.py:87
  158.7 11.1 %collective-permute-start.34 = (bf16[128,1024]{1,0:T(8,128)(2,1)S(1)}, bf16[128,1024]{1,0:T(8,128)(2,1)S(1)}, u32[]{:S(2)}, u32[]{:S(2)}) collective-permute-start(bf16[128,1024]{1,0:T(8,128)(2,1)S(1)} %get-tuple-element.170), channel_id=1, source_target_pairs={{0,8},{1,9},{2,10},{3,11},{4,12},{5,13},{6,14},{7,15},{8,0},{9,1},... | collective-permute-start | bytes 786440 | tf_op jit(solution)/shard_map/ppermute | solution.py:87
  159.1 18.4 %collective-permute-start.35 = (bf16[128,1024]{1,0:T(8,128)(2,1)S(1)}, bf16[128,1024]{1,0:T(8,128)(2,1)S(1)}, u32[]{:S(2)}, u32[]{:S(2)}) collective-permute-start(bf16[128,1024]{1,0:T(8,128)(2,1)S(1)} %get-tuple-element.171), channel_id=1, source_target_pairs={{0,12},{1,13},{2,14},{3,15},{4,8},{5,9},{6,10},{7,11},{8,4},{9,5},... | collective-permute-start | bytes 786440 | tf_op jit(solution)/shard_map/ppermute | solution.py:87
  177.6 8.4 %collective-permute-start.36 = (bf16[12400,128]{1,0:T(8,128)(2,1)S(1)}, bf16[12400,128]{1,0:T(8,128)(2,1)S(1)}, u32[]{:S(2)}, u32[]{:S(2)}) collective-permute-start(bf16[12400,128]{1,0:T(8,128)(2,1)S(1)} %get-tuple-element.180), channel_id=1, source_target_pairs={{0,16},{1,17},{2,18},{3,19},{4,20},{5,21},{6,22},{7,23},{8,24},{9,... | collective-permute-start | bytes 9523208 | tf_op jit(solution)/shard_map/ppermute | solution.py:87
  186.0 22.9 %copy-start.15 = (bf16[2,128,1024]{2,1,0:T(8,128)(2,1)S(1)}, bf16[2,128,1024]{2,1,0:T(8,128)(2,1)}, u32[]{:S(2)}) copy-start(bf16[2,128,1024]{2,1,0:T(8,128)(2,1)} %get-tuple-element.208) | copy-start | bytes 1572868
  186.8 29.2 %collective-permute-start.37 = (bf16[6256,128]{1,0:T(8,128)(2,1)S(1)}, bf16[6256,128]{1,0:T(8,128)(2,1)S(1)}, u32[]{:S(2)}, u32[]{:S(2)}) collective-permute-start(bf16[6256,128]{1,0:T(8,128)(2,1)S(1)} %get-tuple-element.183), channel_id=1, source_target_pairs={{0,2},{1,3},{2,0},{3,1},{4,6},{5,7},{6,4},{7,5},{8,10},{9,11},{10,... | collective-permute-start | bytes 4804616 | tf_op jit(solution)/shard_map/ppermute | solution.py:87
  187.0 12.1 %collective-permute-start.38 = (bf16[128,1024]{1,0:T(8,128)(2,1)S(1)}, bf16[128,1024]{1,0:T(8,128)(2,1)S(1)}, u32[]{:S(2)}, u32[]{:S(2)}) collective-permute-start(bf16[128,1024]{1,0:T(8,128)(2,1)S(1)} %fusion.18.refs_0_), channel_id=1, source_target_pairs={{0,4},{1,5},{2,6},{3,7},{4,0},{5,1},{6,2},{7,3},{8,12},{9,13},{10,... | collective-permute-start | bytes 786440 | tf_op jit(solution)/shard_map/ppermute | solution.py:87
  191.8 9.0 %collective-permute-start.39 = (bf16[128,1024]{1,0:T(8,128)(2,1)S(1)}, bf16[128,1024]{1,0:T(8,128)(2,1)S(1)}, u32[]{:S(2)}, u32[]{:S(2)}) collective-permute-start(bf16[128,1024]{1,0:T(8,128)(2,1)S(1)} %fusion.18.refs_0_), channel_id=1, source_target_pairs={{0,8},{1,9},{2,10},{3,11},{4,12},{5,13},{6,14},{7,15},{8,0},{9,1},... | collective-permute-start | bytes 786440 | tf_op jit(solution)/shard_map/ppermute | solution.py:87
  192.2 16.6 %collective-permute-start.40 = (bf16[128,1024]{1,0:T(8,128)(2,1)S(1)}, bf16[128,1024]{1,0:T(8,128)(2,1)S(1)}, u32[]{:S(2)}, u32[]{:S(2)}) collective-permute-start(bf16[128,1024]{1,0:T(8,128)(2,1)S(1)} %fusion.18.refs_0_), channel_id=1, source_target_pairs={{0,12},{1,13},{2,14},{3,15},{4,8},{5,9},{6,10},{7,11},{8,4},{9,5},... | collective-permute-start | bytes 786440 | tf_op jit(solution)/shard_map/ppermute | solution.py:87
  208.9 22.8 %collective-permute-start.46 = (bf16[2,128,1024]{2,1,0:T(8,128)(2,1)S(1)}, bf16[2,128,1024]{2,1,0:T(8,128)(2,1)S(1)}, u32[]{:S(2)}, u32[]{:S(2)}) collective-permute-start(bf16[2,128,1024]{2,1,0:T(8,128)(2,1)S(1)} %copy-done.15), channel_id=1, source_target_pairs={{0,4},{1,5},{2,6},{3,7},{4,0},{5,1},{6,2},{7,3},{8,12},{9,13},{10,... | collective-permute-start | bytes 1572872 | tf_op jit(solution)/shard_map/ppermute | solution.py:87
  216.4 15.3 %collective-permute-start.41 = (bf16[3184,128]{1,0:T(8,128)(2,1)S(1)}, bf16[3184,128]{1,0:T(8,128)(2,1)S(1)}, u32[]{:S(2)}, u32[]{:S(2)}) collective-permute-start(bf16[3184,128]{1,0:T(8,128)(2,1)S(1)} %get-tuple-element.185), channel_id=1, source_target_pairs={{0,1},{1,0},{2,3},{3,2},{4,5},{5,4},{6,7},{7,6},{8,9},{9,8},{10,11... | collective-permute-start | bytes 2445320 | tf_op jit(solution)/shard_map/ppermute | solution.py:87
  232.0 7.1 %collective-permute-start.47 = (bf16[12400,128]{1,0:T(8,128)(2,1)S(1)}, bf16[12400,128]{1,0:T(8,128)(2,1)S(1)}, u32[]{:S(2)}, u32[]{:S(2)}) collective-permute-start(bf16[12400,128]{1,0:T(8,128)(2,1)S(1)} %get-tuple-element.210), channel_id=1, source_target_pairs={{0,16},{1,17},{2,18},{3,19},{4,20},{5,21},{6,22},{7,23},{8,24},{9,... | collective-permute-start | bytes 9523208 | tf_op jit(solution)/shard_map/ppermute | solution.py:87
  239.8 19.9 %collective-permute-start.48 = (bf16[6256,128]{1,0:T(8,128)(2,1)S(1)}, bf16[6256,128]{1,0:T(8,128)(2,1)S(1)}, u32[]{:S(2)}, u32[]{:S(2)}) collective-permute-start(bf16[6256,128]{1,0:T(8,128)(2,1)S(1)} %get-tuple-element.212), channel_id=1, source_target_pairs={{0,2},{1,3},{2,0},{3,1},{4,6},{5,7},{6,4},{7,5},{8,10},{9,11},{10,... | collective-permute-start | bytes 4804616 | tf_op jit(solution)/shard_map/ppermute | solution.py:87
  241.2 19.0 %collective-permute-start.49 = (bf16[128,1024]{1,0:T(8,128)(2,1)S(1)}, bf16[128,1024]{1,0:T(8,128)(2,1)S(1)}, u32[]{:S(2)}, u32[]{:S(2)}) collective-permute-start(bf16[128,1024]{1,0:T(8,128)(2,1)S(1)} %fusion.29), channel_id=1, source_target_pairs={{0,8},{1,9},{2,10},{3,11},{4,12},{5,13},{6,14},{7,15},{8,0},{9,1},... | collective-permute-start | bytes 786440 | tf_op jit(solution)/shard_map/ppermute | solution.py:87
  241.2 18.9 %collective-permute-start.42 = (bf16[560,128]{1,0:T(8,128)(2,1)S(1)}, bf16[560,128]{1,0:T(8,128)(2,1)S(1)}, u32[]{:S(2)}, u32[]{:S(2)}) collective-permute-start(bf16[560,128]{1,0:T(8,128)(2,1)S(1)} %get-tuple-element.201), channel_id=1, source_target_pairs={{0,4},{1,5},{2,6},{3,7},{4,0},{5,1},{6,2},{7,3},{8,12},{9,13},{10,... | collective-permute-start | bytes 430088 | tf_op jit(solution)/shard_map/ppermute | solution.py:87
  242.7 17.5 %collective-permute-start.43 = (bf16[560,128]{1,0:T(8,128)(2,1)S(1)}, bf16[560,128]{1,0:T(8,128)(2,1)S(1)}, u32[]{:S(2)}, u32[]{:S(2)}) collective-permute-start(bf16[560,128]{1,0:T(8,128)(2,1)S(1)} %get-tuple-element.202), channel_id=1, source_target_pairs={{0,8},{1,9},{2,10},{3,11},{4,12},{5,13},{6,14},{7,15},{8,0},{9,1},... | collective-permute-start | bytes 430088 | tf_op jit(solution)/shard_map/ppermute | solution.py:87
  243.2 17.0 %collective-permute-start.44 = (bf16[560,128]{1,0:T(8,128)(2,1)S(1)}, bf16[560,128]{1,0:T(8,128)(2,1)S(1)}, u32[]{:S(2)}, u32[]{:S(2)}) collective-permute-start(bf16[560,128]{1,0:T(8,128)(2,1)S(1)} %get-tuple-element.203), channel_id=1, source_target_pairs={{0,12},{1,13},{2,14},{3,15},{4,8},{5,9},{6,10},{7,11},{8,4},{9,5},... | collective-permute-start | bytes 430088 | tf_op jit(solution)/shard_map/ppermute | solution.py:87
  260.2 15.8 %collective-permute-start.50 = (bf16[3184,128]{1,0:T(8,128)(2,1)S(1)}, bf16[3184,128]{1,0:T(8,128)(2,1)S(1)}, u32[]{:S(2)}, u32[]{:S(2)}) collective-permute-start(bf16[3184,128]{1,0:T(8,128)(2,1)S(1)} %get-tuple-element.216), channel_id=1, source_target_pairs={{0,1},{1,0},{2,3},{3,2},{4,5},{5,4},{6,7},{7,6},{8,9},{9,8},{10,11... | collective-permute-start | bytes 2445320 | tf_op jit(solution)/shard_map/ppermute | solution.py:87
  261.6 14.4 %collective-permute-start.45 = (bf16[2,128,1024]{2,1,0:T(8,128)(2,1)S(1)}, bf16[2,128,1024]{2,1,0:T(8,128)(2,1)S(1)}, u32[]{:S(2)}, u32[]{:S(2)}) collective-permute-start(bf16[2,128,1024]{2,1,0:T(8,128)(2,1)S(1)} %get-tuple-element.204), channel_id=1, source_target_pairs={{0,4},{1,5},{2,6},{3,7},{4,0},{5,1},{6,2},{7,3},{8,12},{9,13},{10,... | collective-permute-start | bytes 1572872 | tf_op jit(solution)/shard_map/ppermute | solution.py:87
  277.0 5.7 %collective-permute-start.51 = (bf16[560,128]{1,0:T(8,128)(2,1)S(1)}, bf16[560,128]{1,0:T(8,128)(2,1)S(1)}, u32[]{:S(2)}, u32[]{:S(2)}) collective-permute-start(bf16[560,128]{1,0:T(8,128)(2,1)S(1)} %get-tuple-element.219), channel_id=1, source_target_pairs={{0,4},{1,5},{2,6},{3,7},{4,0},{5,1},{6,2},{7,3},{8,12},{9,13},{10,... | collective-permute-start | bytes 430088 | tf_op jit(solution)/shard_map/ppermute | solution.py:87
  277.0 5.7 %collective-permute-start.52 = (bf16[560,128]{1,0:T(8,128)(2,1)S(1)}, bf16[560,128]{1,0:T(8,128)(2,1)S(1)}, u32[]{:S(2)}, u32[]{:S(2)}) collective-permute-start(bf16[560,128]{1,0:T(8,128)(2,1)S(1)} %get-tuple-element.220), channel_id=1, source_target_pairs={{0,8},{1,9},{2,10},{3,11},{4,12},{5,13},{6,14},{7,15},{8,0},{9,1},... | collective-permute-start | bytes 430088 | tf_op jit(solution)/shard_map/ppermute | solution.py:87
  278.8 8.5 %collective-permute-start.53 = (bf16[560,128]{1,0:T(8,128)(2,1)S(1)}, bf16[560,128]{1,0:T(8,128)(2,1)S(1)}, u32[]{:S(2)}, u32[]{:S(2)}) collective-permute-start(bf16[560,128]{1,0:T(8,128)(2,1)S(1)} %get-tuple-element.221), channel_id=1, source_target_pairs={{0,12},{1,13},{2,14},{3,15},{4,8},{5,9},{6,10},{7,11},{8,4},{9,5},... | collective-permute-start | bytes 430088 | tf_op jit(solution)/shard_map/ppermute | solution.py:87
  288.0 5.3 %collective-permute-start.55 = (f32[8,128]{1,0:T(8,128)S(1)}, f32[8,128]{1,0:T(8,128)S(1)}, u32[]{:S(2)}, u32[]{:S(2)}) collective-permute-start(f32[8,128]{1,0:T(8,128)S(1)} %get-tuple-element.226), channel_id=1, source_target_pairs={{0,16},{1,17},{2,18},{3,19},{4,20},{5,21},{6,22},{7,23},{8,24},{9,... | collective-permute-start | bytes 12296 | tf_op jit(solution)/shard_map/ppermute | solution.py:87
  292.5 9.7 %collective-permute-start.58 = (bf16[3072,128]{1,0:T(8,128)(2,1)S(1)}, bf16[3072,128]{1,0:T(8,128)(2,1)S(1)}, u32[]{:S(2)}, u32[]{:S(2)}) collective-permute-start(bf16[3072,128]{1,0:T(8,128)(2,1)S(1)} %get-tuple-element.227), channel_id=1, source_target_pairs={{0,16},{1,17},{2,18},{3,19},{4,20},{5,21},{6,22},{7,23},{8,24},{9,... | collective-permute-start | bytes 2359304 | tf_op jit(solution)/shard_map/ppermute | solution.py:87
  293.3 2.5 collective-permute-start.56
  293.8 8.4 %collective-permute-start.54 = (bf16[128,1024]{1,0:T(8,128)(2,1)S(1)}, bf16[128,1024]{1,0:T(8,128)(2,1)S(1)}, u32[]{:S(2)}, u32[]{:S(2)}) collective-permute-start(bf16[128,1024]{1,0:T(8,128)(2,1)S(1)} %fusion.28), channel_id=1, source_target_pairs={{0,8},{1,9},{2,10},{3,11},{4,12},{5,13},{6,14},{7,15},{8,0},{9,1},... | collective-permute-start | bytes 786440 | tf_op jit(solution)/shard_map/ppermute | solution.py:87
  295.8 2.5 collective-permute-start.57
  304.4 13.1 %collective-permute-start.59 = (bf16[2,128,1024]{2,1,0:T(8,128)(2,1)}, bf16[2,128,1024]{2,1,0:T(8,128)(2,1)}, u32[]{:S(2)}, u32[]{:S(2)}) collective-permute-start(bf16[2,128,1024]{2,1,0:T(8,128)(2,1)} %broadcast_select_fusion.4), channel_id=1, source_target_pairs={{0,16},{1,17},{2,18},{3,19},{4,20},{5,21},{6,22},{7,23},{8,24},{9,... | collective-permute-start | bytes 1572872 | tf_op jit(solution)/shard_map/ppermute | solution.py:87
  (13 other events, 80.9 us)
where the time goes:
time: 326 us; the launch traced here: 321 us
  waiting for transfers between devices  141 us (43%)
  starting transfers between devices  91.6 us (28%)
  Pallas kernels  58.5 us (18%)
  other arithmetic  15.3 us (5%)
  local copies, waits for them, and re-layouts  10.9 us (3%)
  between operations  3.72 us (1%)
    ppermute x60, waiting for transfers between devices, move(): return lax.ppermute(block, AXES, route)  141 us
    ppermute x60, starting transfers between devices, move(): return lax.ppermute(block, AXES, route)  91.6 us
    pallas_call x1, Pallas kernels, middle(): pl.pallas_call(functools.partial(middle_kernel, ring, len(parts)), out_sh...  13.3 us
    pallas_call x1, Pallas kernels, backward(): pl.pallas_call(functools.partial(backward_kernel, ring), out_shape=tuple(...  12.4 us
    pallas_call x1, Pallas kernels, forward(): pl.pallas_call(functools.partial(forward_kernel, ring, len(parts)), out_s...  10.8 us
    pallas_call x1, Pallas kernels, adam(): pl.pallas_call(adam_kernel, grid=(steps,), out_shape=tuple((shaped(a.shap...  8.86 us
  transfers between devices with their start and end apart: 60, of which 28 were waited for; matrix products, arithmetic and copies ran while one was open for 6% of the time, Pallas kernels for 12%

commit v1 on v0

--- a/solution.py
+++ b/solution.py
@@ -1001,9 +1001,9 @@
         qu = jnp.where((core == 0) ^ later, keep_qu, came_qu)
         return [take(qu, group)] + [place.member(take(qu, group ^ r), r) for r in members]
 
-    def gather(block, *waited):
-        late = after(block, *waited)
-        return [block] + [place.member(late, r) for r in members]
+    def gather(block):
+        near = [place.member(block, r) for r in (1, 2)]
+        return [block, *near, place.member(near[1], 1)]
 
     def to_owners(slots):
         return [slots[0]] + [place.member(slots[r], r) for r in members]

time: 326 us -> 316 us (0.969)
  starting transfers between devices: 91.6 us -> 84.5 us
    ppermute x60, starting transfers between devices: 91.6 us -> 84.5 us  [move(): return lax.ppermute(block, AXES, route)]
  transfers between devices with their start and end apart: 60 -> 60, of which waited for: 28 -> 26; matrix products, arithmetic and copies ran while one was open for 6% -> 6% of each run, Pallas kernels for 12% -> 13%
where the time goes in v1:
time: 316 us; the launch traced here: 311 us
  waiting for transfers between devices  139 us (44%)
  starting transfers between devices  84.5 us (27%)
  Pallas kernels  58.5 us (19%)
  other arithmetic  15.3 us (5%)
  local copies, waits for them, and re-layouts  10.9 us (3%)
  between operations  3.72 us (1%)
    ppermute x60, waiting for transfers between devices, move(): return lax.ppermute(block, AXES, route)  139 us
    ppermute x60, starting transfers between devices, move(): return lax.ppermute(block, AXES, route)  84.5 us
    pallas_call x1, Pallas kernels, middle(): pl.pallas_call(functools.partial(middle_kernel, ring, len(parts)), out_sh...  13.3 us
    pallas_call x1, Pallas kernels, backward(): pl.pallas_call(functools.partial(backward_kernel, ring), out_shape=tuple(...  12.4 us
    pallas_call x1, Pallas kernels, forward(): pl.pallas_call(functools.partial(forward_kernel, ring, len(parts)), out_s...  10.8 us
    pallas_call x1, Pallas kernels, adam(): pl.pallas_call(adam_kernel, grid=(steps,), out_shape=tuple((shaped(a.shap...  8.86 us
    pallas_call x1, Pallas kernels, weight_grads(): pl.pallas_call(functools.partial(grads_kernel, ring), out_shape=(out, out...  6.42 us
  transfers between devices with their start and end apart: 60, of which 26 were waited for; matrix products, arithmetic and copies ran while one was open for 6% of the time, Pallas kernels for 13%

profile of v1, /device:TPU:1, one launch (start us, length us, event | category | flops | bytes accessed | tf_op | source)
XLA Modules:
  0.0 311.4 jit_solution(1317841585744004254)
XLA Ops:
  1.6 2.5 pack_weights.1
  6.8 2.3 collective-permute-start.5
  9.1 2.0 broadcast_select_fusion.1
  11.1 3.4 %collective-permute-start.3 = (bf16[64,1024]{1,0:T(8,128)(2,1)S(1)}, bf16[64,1024]{1,0:T(8,128)(2,1)S(1)}, u32[]{:S(2)}, u32[]{:S(2)}) collective-permute-start(bf16[64,1024]{1,0:T(8,128)(2,1)S(1)} %get-tuple-element.275), channel_id=1, source_target_pairs={{0,12},{1,13},{2,14},{3,15},{4,8},{5,9},{6,10},{7,11},{8,4},{9,5},... | collective-permute-start | bytes 393224 | tf_op jit(solution)/shard_map/ppermute | solution.py:87
  15.0 1.3 collective-permute-start.7
  16.2 1.3 collective-permute-done.3
  17.5 4.2 %collective-permute-done.1 = bf16[64,1024]{1,0:T(8,128)(2,1)S(1)} collective-permute-done((bf16[64,1024]{1,0:T(8,128)(2,1)S(1)}, bf16[64,1024]{1,0:T(8,128)(2,1)S(1)}, u32[]{:S(2)}, u32[]{:S(2)}) %collective-permute-start.1) | collective-permute-done | bytes 131104 | tf_op jit(solution)/shard_map/ppermute | solution.py:87
  21.8 3.4 %collective-permute-done.2 = bf16[64,1024]{1,0:T(8,128)(2,1)S(1)} collective-permute-done((bf16[64,1024]{1,0:T(8,128)(2,1)S(1)}, bf16[64,1024]{1,0:T(8,128)(2,1)S(1)}, u32[]{:S(2)}, u32[]{:S(2)}) %collective-permute-start.2) | collective-permute-done | bytes 131104 | tf_op jit(solution)/shard_map/ppermute | solution.py:87
  26.5 7.1 %collective-permute-done.6 = bf16[1,4,64,1024]{3,2,1,0:T(8,128)(2,1)S(1)} collective-permute-done((bf16[1,4,64,1024]{3,2,1,0:T(8,128)(2,1)S(1)}, bf16[1,4,64,1024]{3,2,1,0:T(8,128)(2,1)S(1)}, u32[]{:S(2)}, u32[]{:S(2)}) %collective-permute-start.6) | collective-permute-done | bytes 524320 | tf_op jit(solution)/shard_map/ppermute | solution.py:87
  33.7 2.3 collective-permute-start.9
  35.9 2.6 collective-permute-done.14.refs_10_
  38.6 4.9 %collective-permute-start.8 = (bf16[2,4,64,1024]{3,2,1,0:T(8,128)(2,1)S(1)}, bf16[2,4,64,1024]{3,2,1,0:T(8,128)(2,1)}, u32[]{:S(2)}, u32[]{:S(2)}) collective-permute-start(bf16[2,4,64,1024]{3,2,1,0:T(8,128)(2,1)S(1)} %constant_dynamic-update-slice_fusion.refs_0_), channel_id=1, source_target_pairs={{0,2},{1,3},{2,0},{3,1},{4,6},{5,7},{6,4},{7,5},{8,10},{9,11},{10,... | collective-permute-start | bytes 3145736 | tf_op jit(solution)/shard_map/ppermute | solution.py:87
  43.6 1.8 constant_dynamic-slice_fusion.1
  45.4 1.1 pad_maximum_fusion.7
  48.8 1.5 collective-permute-start.20
  50.7 1.8 collective-permute-start.22
  52.5 3.6 %collective-permute-done.8.refs_1_ = bf16[2,4,64,1024]{3,2,1,0:T(8,128)(2,1)} collective-permute-done((bf16[2,4,64,1024]{3,2,1,0:T(8,128)(2,1)S(1)}, bf16[2,4,64,1024]{3,2,1,0:T(8,128)(2,1)}, u32[]{:S(2)}, u32[]{:S(2)}) %collective-permute-start.8) | collective-permute-done | bytes 1048608 | tf_op jit(solution)/shard_map/ppermute | solution.py:87
  57.5 1.5 gather_fusion
  63.0 10.8 %forward_shard.1 = (bf16[128,1024]{1,0:T(8,128)(2,1)S(1)}, bf16[128,1024]{1,0:T(8,128)(2,1)S(1)}, bf16[128,1024]{1,0:T(8,128)(2,1)S(1)}, bf16[128,1024]{1,0:T(8,...) custom-call(s32[3]{0:T(128)S(1)} %pad_add_fusion.info, ...), custom_call_target="tpu_custom_call" | custom-call | flops 6442450944 | bytes 33554432 | tf_op jit(solution)/shard_map/forward_shard/pallas_call | solution.py:521
  73.9 1.6 collective-permute-start.17
  75.5 1.5 collective-permute-start.16
  77.6 1.3 collective-permute-done.21.refs_14_
  81.3 22.7 %collective-permute-done.18 = bf16[128,1024]{1,0:T(8,128)(2,1)S(1)} collective-permute-done((bf16[128,1024]{1,0:T(8,128)(2,1)S(1)}, bf16[128,1024]{1,0:T(8,128)(2,1)S(1)}, u32[]{:S(2)}, u32[]{:S(2)}) %collective-permute-start.18) | collective-permute-done | bytes 262176 | tf_op jit(solution)/shard_map/ppermute | solution.py:87
  104.6 2.4 collective-permute-start.24
  107.0 6.2 %collective-permute-start.26 = (bf16[128,1024]{1,0:T(8,128)(2,1)S(1)}, bf16[128,1024]{1,0:T(8,128)(2,1)S(1)}, u32[]{:S(2)}, u32[]{:S(2)}) collective-permute-start(bf16[128,1024]{1,0:T(8,128)(2,1)S(1)} %get-tuple-element.261.refs_8_), channel_id=1, source_target_pairs={{0,8},{1,9},{2,10},{3,11},{4,12},{5,13},{6,14},{7,15},{8,0},{9,1},... | collective-permute-start | bytes 786440 | tf_op jit(solution)/shard_map/ppermute | solution.py:87
  113.2 9.3 %collective-permute-done.26.refs_10_ = bf16[128,1024]{1,0:T(8,128)(2,1)S(1)} collective-permute-done((bf16[128,1024]{1,0:T(8,128)(2,1)S(1)}, bf16[128,1024]{1,0:T(8,128)(2,1)S(1)}, u32[]{:S(2)}, u32[]{:S(2)}) %collective-permute-start.26) | collective-permute-done | bytes 262176 | tf_op jit(solution)/shard_map/ppermute | solution.py:87
  122.5 6.2 %collective-permute-done.27.refs_11_ = bf16[128,1024]{1,0:T(8,128)(2,1)S(1)} collective-permute-done((bf16[128,1024]{1,0:T(8,128)(2,1)S(1)}, bf16[128,1024]{1,0:T(8,128)(2,1)S(1)}, u32[]{:S(2)}, u32[]{:S(2)}) %collective-permute-start.27) | collective-permute-done | bytes 262176 | tf_op jit(solution)/shard_map/ppermute | solution.py:87
  128.7 3.8 %collective-permute-start.29 = (bf16[2,4,64,1024]{3,2,1,0:T(8,128)(2,1)S(1)}, bf16[2,4,64,1024]{3,2,1,0:T(8,128)(2,1)S(1)}, u32[]{:S(2)}, u32[]{:S(2)}) collective-permute-start(bf16[2,4,64,1024]{3,2,1,0:T(8,128)(2,1)S(1)} %pad_maximum_fusion.refs_0_), channel_id=1, source_target_pairs={{0,16},{1,17},{2,18},{3,19},{4,20},{5,21},{6,22},{7,23},{8,24},{9,... | collective-permute-start | bytes 3145736 | tf_op jit(solution)/shard_map/ppermute | solution.py:87
  133.0 3.7 %collective-permute-start.32 = (bf16[2,320,512]{2,1,0:T(8,128)(2,1)S(1)}, bf16[2,320,512]{2,1,0:T(8,128)(2,1)S(1)}, u32[]{:S(2)}, u32[]{:S(2)}) collective-permute-start(bf16[2,320,512]{2,1,0:T(8,128)(2,1)S(1)} %collective-permute-done.28.refs_3_), channel_id=1, source_target_pairs={{0,16},{1,17},{2,18},{3,19},{4,20},{5,21},{6,22},{7,23},{8,24},{9,... | collective-permute-start | bytes 1966088 | tf_op jit(solution)/shard_map/ppermute | solution.py:87
  137.2 1.2 collective-permute-done.32.refs_7_
  138.4 13.3 %forward_backward_shard.1 = (bf16[128,1024]{1,0:T(8,128)(2,1)S(1)}, bf16[128,1024]{1,0:T(8,128)(2,1)S(1)}, bf16[128,1024]{1,0:T(8,128)(2,1)S(1)}, bf16[128,1024]...) custom-call(s32[3]{0:T(128)S(1)} %pad_add_fusion.info, ...), custom_call_target="tpu_custom_call" | custom-call | flops 12884901888 | bytes 33554432 | tf_op jit(solution)/shard_map/forward_backward_shard/pallas_call | solution.py:583
  151.8 1.8 collective-permute-start.33
  154.3 1.5 collective-permute-start.35
  155.7 6.4 %weight_grads.1 = (bf16[12400,128]{1,0:T(8,128)(2,1)S(1)}, bf16[12400,128]{1,0:T(8,128)(2,1)S(1)}) custom-call(s32[3]{0:T(128)S(1)} %pad_add_fusion.info, bf16[512,256]{1,0:T(8,128)(2,1)} %get-tuple-element.172.far_mixed, bf16[512,1024]{1,0:T(8,128)(2,1)} %get-tuple-element.173.far_active, bf16[512,1024]{1,0:T(8,128)(2,1)} %get-tuple-element.174.far_grad, ...), custom_call_target="tpu_custom_call" | custom-call | flops 99999997952 | bytes 25165824 | tf_op jit(solution)/shard_map/weight_grads/pallas_call | solution.py:742
  162.2 2.6 collective-permute-done.33
  164.8 7.9 %collective-permute-done.35 = bf16[128,1024]{1,0:T(8,128)(2,1)S(1)} collective-permute-done((bf16[128,1024]{1,0:T(8,128)(2,1)S(1)}, bf16[128,1024]{1,0:T(8,128)(2,1)S(1)}, u32[]{:S(2)}, u32[]{:S(2)}) %collective-permute-start.35) | collective-permute-done | bytes 262176 | tf_op jit(solution)/shard_map/ppermute | solution.py:87
  172.7 2.9 collective-permute-start.36
  176.4 4.5 %collective-permute-done.36.came = bf16[12400,128]{1,0:T(8,128)(2,1)S(1)} collective-permute-done((bf16[12400,128]{1,0:T(8,128)(2,1)S(1)}, bf16[12400,128]{1,0:T(8,128)(2,1)S(1)}, u32[]{:S(2)}, u32[]{:S(2)}) %collective-permute-start.36) | collective-permute-done | bytes 3174432 | tf_op jit(solution)/shard_map/ppermute | solution.py:87
  181.9 5.4 %collective-permute-start.39 = (bf16[128,1024]{1,0:T(8,128)(2,1)S(1)}, bf16[128,1024]{1,0:T(8,128)(2,1)S(1)}, u32[]{:S(2)}, u32[]{:S(2)}) collective-permute-start(bf16[128,1024]{1,0:T(8,128)(2,1)S(1)} %fusion.18.refs_0_), channel_id=1, source_target_pairs={{0,8},{1,9},{2,10},{3,11},{4,12},{5,13},{6,14},{7,15},{8,0},{9,1},... | collective-permute-start | bytes 786440 | tf_op jit(solution)/shard_map/ppermute | solution.py:87
  187.3 10.7 %collective-permute-done.39.refs_2_ = bf16[128,1024]{1,0:T(8,128)(2,1)S(1)} collective-permute-done((bf16[128,1024]{1,0:T(8,128)(2,1)S(1)}, bf16[128,1024]{1,0:T(8,128)(2,1)S(1)}, u32[]{:S(2)}, u32[]{:S(2)}) %collective-permute-start.39) | collective-permute-done | bytes 262176 | tf_op jit(solution)/shard_map/ppermute | solution.py:87
  198.0 5.6 %collective-permute-done.40.refs_3_ = bf16[128,1024]{1,0:T(8,128)(2,1)S(1)} collective-permute-done((bf16[128,1024]{1,0:T(8,128)(2,1)S(1)}, bf16[128,1024]{1,0:T(8,128)(2,1)S(1)}, u32[]{:S(2)}, u32[]{:S(2)}) %collective-permute-start.40) | collective-permute-done | bytes 262176 | tf_op jit(solution)/shard_map/ppermute | solution.py:87
  203.6 1.8 collective-permute-start.46
  205.8 2.6 collective-permute-start.41
  208.4 12.4 %backward_shard.1 = (bf16[2,128,1024]{2,1,0:T(8,128)(2,1)S(1)}, bf16[2,128,1024]{2,1,0:T(8,128)(2,1)S(1)}, bf16[12400,128]{1,0:T(8,128)(2,1)S(1)}, bf16[12400,128]{1,0:T(8,128)(2,1)S(1)}) custom-call(s32[3]{0:T(128)S(1)} %pad_add_fusion.info, bf16[128,1024]{1,0:T(8,128)(2,1)S(1)} %fusion.18.refs_0_, bf16[128,1024]{1,0:T(8,128)(2,1)S(1)} %collective-permute-done.38.refs_1_, ...), custom_call_target="tpu_custom_call" | custom-call | flops 12884901888 | bytes 33554432 | tf_op jit(solution)/shard_map/backward_shard/pallas_call | solution.py:637
  221.2 1.4 collective-permute-start.47
  222.6 5.3 %collective-permute-done.47.came = bf16[12400,128]{1,0:T(8,128)(2,1)S(1)} collective-permute-done((bf16[12400,128]{1,0:T(8,128)(2,1)S(1)}, bf16[12400,128]{1,0:T(8,128)(2,1)S(1)}, u32[]{:S(2)}, u32[]{:S(2)}) %collective-permute-start.47) | collective-permute-done | bytes 3174432 | tf_op jit(solution)/shard_map/ppermute | solution.py:87
  228.6 1.3 collective-permute-start.48
  231.5 1.9 collective-permute-start.43
  233.4 1.2 collective-permute-start.44
  234.6 13.9 %collective-permute-done.48.came = bf16[6256,128]{1,0:T(8,128)(2,1)S(1)} collective-permute-done((bf16[6256,128]{1,0:T(8,128)(2,1)S(1)}, bf16[6256,128]{1,0:T(8,128)(2,1)S(1)}, u32[]{:S(2)}, u32[]{:S(2)}) %collective-permute-start.48) | collective-permute-done | bytes 1601568 | tf_op jit(solution)/shard_map/ppermute | solution.py:87
  249.0 2.0 collective-permute-start.50
  251.0 1.5 collective-permute-start.45
  252.6 13.0 %collective-permute-done.45 = bf16[2,128,1024]{2,1,0:T(8,128)(2,1)S(1)} collective-permute-done((bf16[2,128,1024]{2,1,0:T(8,128)(2,1)S(1)}, bf16[2,128,1024]{2,1,0:T(8,128)(2,1)S(1)}, u32[]{:S(2)}, u32[]{:S(2)}) %collective-permute-start.45) | collective-permute-done | bytes 524320 | tf_op jit(solution)/shard_map/ppermute | solution.py:87
  266.6 1.6 collective-permute-start.52
  268.2 1.9 collective-permute-start.53
  270.1 4.2 %collective-permute-done.51.refs_1_ = bf16[560,128]{1,0:T(8,128)(2,1)S(1)} collective-permute-done((bf16[560,128]{1,0:T(8,128)(2,1)S(1)}, bf16[560,128]{1,0:T(8,128)(2,1)S(1)}, u32[]{:S(2)}, u32[]{:S(2)}) %collective-permute-start.51) | collective-permute-done | bytes 143392 | tf_op jit(solution)/shard_map/ppermute | solution.py:87
  274.3 2.8 collective-permute-done.53.refs_3_
  277.7 4.4 %collective-permute-start.55 = (f32[8,128]{1,0:T(8,128)S(1)}, f32[8,128]{1,0:T(8,128)S(1)}, u32[]{:S(2)}, u32[]{:S(2)}) collective-permute-start(f32[8,128]{1,0:T(8,128)S(1)} %get-tuple-element.226), channel_id=1, source_target_pairs={{0,16},{1,17},{2,18},{3,19},{4,20},{5,21},{6,22},{7,23},{8,24},{9,... | collective-permute-start | bytes 12296 | tf_op jit(solution)/shard_map/ppermute | solution.py:87
  283.1 1.9 collective-permute-start.54
  285.4 1.2 collective-permute-start.57
  288.4 2.3 collective-permute-done.54
  293.0 4.3 %collective-permute-start.59 = (bf16[2,128,1024]{2,1,0:T(8,128)(2,1)}, bf16[2,128,1024]{2,1,0:T(8,128)(2,1)}, u32[]{:S(2)}, u32[]{:S(2)}) collective-permute-start(bf16[2,128,1024]{2,1,0:T(8,128)(2,1)} %broadcast_select_fusion.4), channel_id=1, source_target_pairs={{0,16},{1,17},{2,18},{3,19},{4,20},{5,21},{6,22},{7,23},{8,24},{9,... | collective-permute-start | bytes 1572872 | tf_op jit(solution)/shard_map/ppermute | solution.py:87
  298.7 8.9 %adamw.1 = (f32[1,64,3072]{2,1,0:T(8,128)}, f32[1,64,3072]{2,1,0:T(8,128)}, f32[1,64,3072]{2,1,0:T(8,128)}, f32[1,64,1024]{2,1,0:T(8,128)}, f32[1,64,1024]{2,1,0...) custom-call(s32[3]{0:T(128)S(1)} %pad_add_fusion.info, ...), custom_call_target="tpu_custom_call" | custom-call | tf_op jit(solution)/shard_map/adamw/pallas_call | solution.py:933
  307.6 1.2 broadcast_select_fusion
  (195 shorter events, 32.8 us)
Async XLA Ops:
  4.1 1.9 collective-permute-start.4
  4.2 4.9 %collective-permute-start = (bf16[4,64,1024]{2,1,0:T(8,128)(2,1)S(1)}, bf16[4,64,1024]{2,1,0:T(8,128)(2,1)}, u32[]{:S(2)}, u32[]{:S(2)}) collective-permute-start(bf16[4,64,1024]{2,1,0:T(8,128)(2,1)S(1)} %get-tuple-element.138), channel_id=1, source_target_pairs={{0,16},{1,17},{2,18},{3,19},{4,20},{5,21},{6,22},{7,23},{8,24},{9,... | collective-permute-start | bytes 1572872 | tf_op jit(solution)/shard_map/ppermute | solution.py:87
  5.8 39.6 %copy-start.7 = (bf16[128,1024]{1,0:T(8,128)(2,1)}, bf16[128,1024]{1,0:T(8,128)(2,1)S(1)}, u32[]{:S(2)}) copy-start(bf16[128,1024]{1,0:T(8,128)(2,1)S(1)} %dynamic-slice_bitcast_fusion.refs_12_) | copy-start | bytes 786436
  6.8 8.1 %collective-permute-start.5 = (bf16[1,320,512]{2,1,0:T(8,128)(2,1)S(1)}, bf16[1,320,512]{2,1,0:T(8,128)(2,1)S(1)}, u32[]{:S(2)}, u32[]{:S(2)}) collective-permute-start(bf16[1,320,512]{2,1,0:T(8,128)(2,1)S(1)} %get-tuple-element.269), channel_id=1, source_target_pairs={{0,1},{1,0},{2,3},{3,2},{4,5},{5,4},{6,7},{7,6},{8,9},{9,8},{10,11... | collective-permute-start | bytes 983048 | tf_op jit(solution)/shard_map/ppermute | solution.py:87
  11.1 6.4 %collective-permute-start.3 = (bf16[64,1024]{1,0:T(8,128)(2,1)S(1)}, bf16[64,1024]{1,0:T(8,128)(2,1)S(1)}, u32[]{:S(2)}, u32[]{:S(2)}) collective-permute-start(bf16[64,1024]{1,0:T(8,128)(2,1)S(1)} %get-tuple-element.275), channel_id=1, source_target_pairs={{0,12},{1,13},{2,14},{3,15},{4,8},{5,9},{6,10},{7,11},{8,4},{9,5},... | collective-permute-start | bytes 393224 | tf_op jit(solution)/shard_map/ppermute | solution.py:87
  14.5 7.3 %collective-permute-start.1 = (bf16[64,1024]{1,0:T(8,128)(2,1)S(1)}, bf16[64,1024]{1,0:T(8,128)(2,1)S(1)}, u32[]{:S(2)}, u32[]{:S(2)}) collective-permute-start(bf16[64,1024]{1,0:T(8,128)(2,1)S(1)} %get-tuple-element.277), channel_id=1, source_target_pairs={{0,4},{1,5},{2,6},{3,7},{4,0},{5,1},{6,2},{7,3},{8,12},{9,13},{10,... | collective-permute-start | bytes 393224 | tf_op jit(solution)/shard_map/ppermute | solution.py:87
  14.5 10.7 %collective-permute-start.2 = (bf16[64,1024]{1,0:T(8,128)(2,1)S(1)}, bf16[64,1024]{1,0:T(8,128)(2,1)S(1)}, u32[]{:S(2)}, u32[]{:S(2)}) collective-permute-start(bf16[64,1024]{1,0:T(8,128)(2,1)S(1)} %get-tuple-element.276), channel_id=1, source_target_pairs={{0,8},{1,9},{2,10},{3,11},{4,12},{5,13},{6,14},{7,15},{8,0},{9,1},... | collective-permute-start | bytes 393224 | tf_op jit(solution)/shard_map/ppermute | solution.py:87
  15.0 23.6 %collective-permute-start.7 = (bf16[2,320,512]{2,1,0:T(8,128)(2,1)S(1)}, bf16[2,320,512]{2,1,0:T(8,128)(2,1)}, u32[]{:S(2)}, u32[]{:S(2)}) collective-permute-start(bf16[2,320,512]{2,1,0:T(8,128)(2,1)S(1)} %pad_maximum_fusion.1.refs_2_), channel_id=1, source_target_pairs={{0,2},{1,3},{2,0},{3,1},{4,6},{5,7},{6,4},{7,5},{8,10},{9,11},{10,... | collective-permute-start | bytes 1966088 | tf_op jit(solution)/shard_map/ppermute | solution.py:87
  25.2 8.4 %collective-permute-start.6 = (bf16[1,4,64,1024]{3,2,1,0:T(8,128)(2,1)S(1)}, bf16[1,4,64,1024]{3,2,1,0:T(8,128)(2,1)S(1)}, u32[]{:S(2)}, u32[]{:S(2)}) collective-permute-start(bf16[1,4,64,1024]{3,2,1,0:T(8,128)(2,1)S(1)} %maximum_bitcast_fusion), channel_id=1, source_target_pairs={{0,1},{1,0},{2,3},{3,2},{4,5},{5,4},{6,7},{7,6},{8,9},{9,8},{10,11... | collective-permute-start | bytes 1572872 | tf_op jit(solution)/shard_map/ppermute | solution.py:87
  25.5 13.1 %collective-permute-start.14 = (bf16[144,1024]{1,0:T(8,128)(2,1)S(1)}, bf16[144,1024]{1,0:T(8,128)(2,1)S(1)}, u32[]{:S(2)}, u32[]{:S(2)}) collective-permute-start(bf16[144,1024]{1,0:T(8,128)(2,1)S(1)} %fusion.27.refs_8_), channel_id=1, source_target_pairs={{0,8},{1,9},{2,10},{3,11},{4,12},{5,13},{6,14},{7,15},{8,0},{9,1},... | collective-permute-start | bytes 884744 | tf_op jit(solution)/shard_map/ppermute | solution.py:87
  25.7 20.8 %collective-permute-start.13 = (bf16[144,1024]{1,0:T(8,128)(2,1)S(1)}, bf16[144,1024]{1,0:T(8,128)(2,1)S(1)}, u32[]{:S(2)}, u32[]{:S(2)}) collective-permute-start(bf16[144,1024]{1,0:T(8,128)(2,1)S(1)} %fusion.27.refs_8_), channel_id=1, source_target_pairs={{0,4},{1,5},{2,6},{3,7},{4,0},{5,1},{6,2},{7,3},{8,12},{9,13},{10,... | collective-permute-start | bytes 884744 | tf_op jit(solution)/shard_map/ppermute | solution.py:87
  33.7 15.1 %collective-permute-start.9 = (bf16[2,4,64,1024]{3,2,1,0:T(8,128)(2,1)S(1)}, bf16[2,4,64,1024]{3,2,1,0:T(8,128)(2,1)}, u32[]{:S(2)}, u32[]{:S(2)}) collective-permute-start(bf16[2,4,64,1024]{3,2,1,0:T(8,128)(2,1)S(1)} %constant_dynamic-update-slice_fusion.refs_0_), channel_id=1, source_target_pairs={{0,16},{1,17},{2,18},{3,19},{4,20},{5,21},{6,22},{7,23},{8,24},{9,... | collective-permute-start | bytes 3145736 | tf_op jit(solution)/shard_map/ppermute | solution.py:87
  38.6 8.5 %collective-permute-start.15 = (bf16[144,1024]{1,0:T(8,128)(2,1)S(1)}, bf16[144,1024]{1,0:T(8,128)(2,1)S(1)}, u32[]{:S(2)}, u32[]{:S(2)}) collective-permute-start(bf16[144,1024]{1,0:T(8,128)(2,1)S(1)} %collective-permute-done.14.refs_10_), channel_id=1, source_target_pairs={{0,4},{1,5},{2,6},{3,7},{4,0},{5,1},{6,2},{7,3},{8,12},{9,13},{10,... | collective-permute-start | bytes 884744 | tf_op jit(solution)/shard_map/ppermute | solution.py:87
  38.6 17.5 %collective-permute-start.8 = (bf16[2,4,64,1024]{3,2,1,0:T(8,128)(2,1)S(1)}, bf16[2,4,64,1024]{3,2,1,0:T(8,128)(2,1)}, u32[]{:S(2)}, u32[]{:S(2)}) collective-permute-start(bf16[2,4,64,1024]{3,2,1,0:T(8,128)(2,1)S(1)} %constant_dynamic-update-slice_fusion.refs_0_), channel_id=1, source_target_pairs={{0,2},{1,3},{2,0},{3,1},{4,6},{5,7},{6,4},{7,5},{8,10},{9,11},{10,... | collective-permute-start | bytes 3145736 | tf_op jit(solution)/shard_map/ppermute | solution.py:87
  46.5 2.3 collective-permute-start.11
  46.5 15.5 %collective-permute-start.12 = (bf16[2,320,512]{2,1,0:T(8,128)(2,1)}, bf16[2,320,512]{2,1,0:T(8,128)(2,1)}, u32[]{:S(2)}, u32[]{:S(2)}) collective-permute-start(bf16[2,320,512]{2,1,0:T(8,128)(2,1)} %collective-permute-done.7.refs_3_), channel_id=1, source_target_pairs={{0,16},{1,17},{2,18},{3,19},{4,20},{5,21},{6,22},{7,23},{8,24},{9,... | collective-permute-start | bytes 1966088 | tf_op jit(solution)/shard_map/ppermute | solution.py:87
  48.8 28.1 %collective-permute-start.20 = (bf16[192,1024]{1,0:T(8,128)(2,1)}, bf16[192,1024]{1,0:T(8,128)(2,1)}, u32[]{:S(2)}, u32[]{:S(2)}) collective-permute-start(bf16[192,1024]{1,0:T(8,128)(2,1)} %get-tuple-element.152), channel_id=1, source_target_pairs={{0,4},{1,5},{2,6},{3,7},{4,0},{5,1},{6,2},{7,3},{8,12},{9,13},{10,... | collective-permute-start | bytes 1179656 | tf_op jit(solution)/shard_map/ppermute | solution.py:87
  50.3 28.5 %collective-permute-start.21 = (bf16[192,1024]{1,0:T(8,128)(2,1)}, bf16[192,1024]{1,0:T(8,128)(2,1)}, u32[]{:S(2)}, u32[]{:S(2)}) collective-permute-start(bf16[192,1024]{1,0:T(8,128)(2,1)} %get-tuple-element.154), channel_id=1, source_target_pairs={{0,8},{1,9},{2,10},{3,11},{4,12},{5,13},{6,14},{7,15},{8,0},{9,1},... | collective-permute-start | bytes 1179656 | tf_op jit(solution)/shard_map/ppermute | solution.py:87
  50.7 29.2 %collective-permute-start.22 = (bf16[192,1024]{1,0:T(8,128)(2,1)}, bf16[192,1024]{1,0:T(8,128)(2,1)}, u32[]{:S(2)}, u32[]{:S(2)}) collective-permute-start(bf16[192,1024]{1,0:T(8,128)(2,1)} %get-tuple-element.156), channel_id=1, source_target_pairs={{0,12},{1,13},{2,14},{3,15},{4,8},{5,9},{6,10},{7,11},{8,4},{9,5},... | collective-permute-start | bytes 1179656 | tf_op jit(solution)/shard_map/ppermute | solution.py:87
  56.1 6.0 %collective-permute-start.10 = (bf16[2,4,64,1024]{3,2,1,0:T(8,128)(2,1)}, bf16[2,4,64,1024]{3,2,1,0:T(8,128)(2,1)}, u32[]{:S(2)}, u32[]{:S(2)}) collective-permute-start(bf16[2,4,64,1024]{3,2,1,0:T(8,128)(2,1)} %collective-permute-done.8.refs_1_), channel_id=1, source_target_pairs={{0,16},{1,17},{2,18},{3,19},{4,20},{5,21},{6,22},{7,23},{8,24},{9,... | collective-permute-start | bytes 3145736 | tf_op jit(solution)/shard_map/ppermute | solution.py:87
  63.0 17.9 %copy-start.11 = (bf16[1,64,1024]{2,1,0:T(8,128)(2,1)S(1)}, bf16[1,64,1024]{2,1,0:T(8,128)(2,1)}, u32[]{:S(2)}) copy-start(bf16[1,64,1024]{2,1,0:T(8,128)(2,1)} %get-tuple-element.270) | copy-start | bytes 393220
  73.9 30.2 %copy-start.3 = (bf16[128,1024]{1,0:T(8,128)(2,1)S(1)}, bf16[128,1024]{1,0:T(8,128)(2,1)}, u32[]{:S(2)}) copy-start(bf16[128,1024]{1,0:T(8,128)(2,1)} %copy-done.2) | copy-start | bytes 786436
  73.9 30.1 %collective-permute-start.17 = (bf16[1,320,512]{2,1,0:T(8,128)(2,1)S(1)}, bf16[1,320,512]{2,1,0:T(8,128)(2,1)S(1)}, u32[]{:S(2)}, u32[]{:S(2)}) collective-permute-start(bf16[1,320,512]{2,1,0:T(8,128)(2,1)S(1)} %copy-done.6), channel_id=1, source_target_pairs={{0,1},{1,0},{2,3},{3,2},{4,5},{5,4},{6,7},{7,6},{8,9},{9,8},{10,11... | collective-permute-start | bytes 983048 | tf_op jit(solution)/shard_map/ppermute | solution.py:87
  75.5 28.6 %collective-permute-start.16 = (bf16[128,1024]{1,0:T(8,128)(2,1)S(1)}, bf16[128,1024]{1,0:T(8,128)(2,1)S(1)}, u32[]{:S(2)}, u32[]{:S(2)}) collective-permute-start(bf16[128,1024]{1,0:T(8,128)(2,1)S(1)} %get-tuple-element.146), channel_id=1, source_target_pairs={{0,4},{1,5},{2,6},{3,7},{4,0},{5,1},{6,2},{7,3},{8,12},{9,13},{10,... | collective-permute-start | bytes 786440 | tf_op jit(solution)/shard_map/ppermute | solution.py:87
  76.9 27.1 %collective-permute-start.18 = (bf16[128,1024]{1,0:T(8,128)(2,1)S(1)}, bf16[128,1024]{1,0:T(8,128)(2,1)S(1)}, u32[]{:S(2)}, u32[]{:S(2)}) collective-permute-start(bf16[128,1024]{1,0:T(8,128)(2,1)S(1)} %get-tuple-element.149), channel_id=1, source_target_pairs={{0,8},{1,9},{2,10},{3,11},{4,12},{5,13},{6,14},{7,15},{8,0},{9,1},... | collective-permute-start | bytes 786440 | tf_op jit(solution)/shard_map/ppermute | solution.py:87
  78.9 25.2 %collective-permute-start.19 = (bf16[128,1024]{1,0:T(8,128)(2,1)S(1)}, bf16[128,1024]{1,0:T(8,128)(2,1)S(1)}, u32[]{:S(2)}, u32[]{:S(2)}) collective-permute-start(bf16[128,1024]{1,0:T(8,128)(2,1)S(1)} %get-tuple-element.151), channel_id=1, source_target_pairs={{0,12},{1,13},{2,14},{3,15},{4,8},{5,9},{6,10},{7,11},{8,4},{9,5},... | collective-permute-start | bytes 786440 | tf_op jit(solution)/shard_map/ppermute | solution.py:87
  81.0 23.4 %collective-permute-start.23 = (bf16[1,4,64,1024]{3,2,1,0:T(8,128)(2,1)S(1)}, bf16[1,4,64,1024]{3,2,1,0:T(8,128)(2,1)S(1)}, u32[]{:S(2)}, u32[]{:S(2)}) collective-permute-start(bf16[1,4,64,1024]{3,2,1,0:T(8,128)(2,1)S(1)} %maximum_bitcast_fusion.1), channel_id=1, source_target_pairs={{0,1},{1,0},{2,3},{3,2},{4,5},{5,4},{6,7},{7,6},{8,9},{9,8},{10,11... | collective-permute-start | bytes 1572872 | tf_op jit(solution)/shard_map/ppermute | solution.py:87
  104.6 27.9 %collective-permute-start.24 = (bf16[2,4,64,1024]{3,2,1,0:T(8,128)(2,1)S(1)}, bf16[2,4,64,1024]{3,2,1,0:T(8,128)(2,1)S(1)}, u32[]{:S(2)}, u32[]{:S(2)}) collective-permute-start(bf16[2,4,64,1024]{3,2,1,0:T(8,128)(2,1)S(1)} %pad_maximum_fusion.refs_0_), channel_id=1, source_target_pairs={{0,2},{1,3},{2,0},{3,1},{4,6},{5,7},{6,4},{7,5},{8,10},{9,11},{10,... | collective-permute-start | bytes 3145736 | tf_op jit(solution)/shard_map/ppermute | solution.py:87
  107.0 15.5 %collective-permute-start.26 = (bf16[128,1024]{1,0:T(8,128)(2,1)S(1)}, bf16[128,1024]{1,0:T(8,128)(2,1)S(1)}, u32[]{:S(2)}, u32[]{:S(2)}) collective-permute-start(bf16[128,1024]{1,0:T(8,128)(2,1)S(1)} %get-tuple-element.261.refs_8_), channel_id=1, source_target_pairs={{0,8},{1,9},{2,10},{3,11},{4,12},{5,13},{6,14},{7,15},{8,0},{9,1},... | collective-permute-start | bytes 786440 | tf_op jit(solution)/shard_map/ppermute | solution.py:87
  113.2 9.3 %collective-permute-start.25 = (bf16[128,1024]{1,0:T(8,128)(2,1)S(1)}, bf16[128,1024]{1,0:T(8,128)(2,1)S(1)}, u32[]{:S(2)}, u32[]{:S(2)}) collective-permute-start(bf16[128,1024]{1,0:T(8,128)(2,1)S(1)} %get-tuple-element.261.refs_8_), channel_id=1, source_target_pairs={{0,4},{1,5},{2,6},{3,7},{4,0},{5,1},{6,2},{7,3},{8,12},{9,13},{10,... | collective-permute-start | bytes 786440 | tf_op jit(solution)/shard_map/ppermute | solution.py:87
  122.5 6.2 %collective-permute-start.27 = (bf16[128,1024]{1,0:T(8,128)(2,1)S(1)}, bf16[128,1024]{1,0:T(8,128)(2,1)S(1)}, u32[]{:S(2)}, u32[]{:S(2)}) collective-permute-start(bf16[128,1024]{1,0:T(8,128)(2,1)S(1)} %collective-permute-done.26.refs_10_), channel_id=1, source_target_pairs={{0,4},{1,5},{2,6},{3,7},{4,0},{5,1},{6,2},{7,3},{8,12},{9,13},{10,... | collective-permute-start | bytes 786440 | tf_op jit(solution)/shard_map/ppermute | solution.py:87
  122.5 10.5 %collective-permute-start.28 = (bf16[2,320,512]{2,1,0:T(8,128)(2,1)S(1)}, bf16[2,320,512]{2,1,0:T(8,128)(2,1)S(1)}, u32[]{:S(2)}, u32[]{:S(2)}) collective-permute-start(bf16[2,320,512]{2,1,0:T(8,128)(2,1)S(1)} %constant_dynamic-update-slice_fusion.2.refs_2_), channel_id=1, source_target_pairs={{0,2},{1,3},{2,0},{3,1},{4,6},{5,7},{6,4},{7,5},{8,10},{9,11},{10,... | collective-permute-start | bytes 1966088 | tf_op jit(solution)/shard_map/ppermute | solution.py:87
  128.7 9.8 %collective-permute-start.29 = (bf16[2,4,64,1024]{3,2,1,0:T(8,128)(2,1)S(1)}, bf16[2,4,64,1024]{3,2,1,0:T(8,128)(2,1)S(1)}, u32[]{:S(2)}, u32[]{:S(2)}) collective-permute-start(bf16[2,4,64,1024]{3,2,1,0:T(8,128)(2,1)S(1)} %pad_maximum_fusion.refs_0_), channel_id=1, source_target_pairs={{0,16},{1,17},{2,18},{3,19},{4,20},{5,21},{6,22},{7,23},{8,24},{9,... | collective-permute-start | bytes 3145736 | tf_op jit(solution)/shard_map/ppermute | solution.py:87
  132.5 5.9 %collective-permute-start.30 = (bf16[2,4,64,1024]{3,2,1,0:T(8,128)(2,1)S(1)}, bf16[2,4,64,1024]{3,2,1,0:T(8,128)(2,1)S(1)}, u32[]{:S(2)}, u32[]{:S(2)}) collective-permute-start(bf16[2,4,64,1024]{3,2,1,0:T(8,128)(2,1)S(1)} %collective-permute-done.24.refs_1_), channel_id=1, source_target_pairs={{0,16},{1,17},{2,18},{3,19},{4,20},{5,21},{6,22},{7,23},{8,24},{9,... | collective-permute-start | bytes 3145736 | tf_op jit(solution)/shard_map/ppermute | solution.py:87
  132.5 4.7 %collective-permute-start.31 = (bf16[2,320,512]{2,1,0:T(8,128)(2,1)S(1)}, bf16[2,320,512]{2,1,0:T(8,128)(2,1)S(1)}, u32[]{:S(2)}, u32[]{:S(2)}) collective-permute-start(bf16[2,320,512]{2,1,0:T(8,128)(2,1)S(1)} %constant_dynamic-update-slice_fusion.2.refs_2_), channel_id=1, source_target_pairs={{0,16},{1,17},{2,18},{3,19},{4,20},{5,21},{6,22},{7,23},{8,24},{9,... | collective-permute-start | bytes 1966088 | tf_op jit(solution)/shard_map/ppermute | solution.py:87
  133.0 5.4 %collective-permute-start.32 = (bf16[2,320,512]{2,1,0:T(8,128)(2,1)S(1)}, bf16[2,320,512]{2,1,0:T(8,128)(2,1)S(1)}, u32[]{:S(2)}, u32[]{:S(2)}) collective-permute-start(bf16[2,320,512]{2,1,0:T(8,128)(2,1)S(1)} %collective-permute-done.28.refs_3_), channel_id=1, source_target_pairs={{0,16},{1,17},{2,18},{3,19},{4,20},{5,21},{6,22},{7,23},{8,24},{9,... | collective-permute-start | bytes 1966088 | tf_op jit(solution)/shard_map/ppermute | solution.py:87
  151.8 13.0 %collective-permute-start.33 = (bf16[128,1024]{1,0:T(8,128)(2,1)S(1)}, bf16[128,1024]{1,0:T(8,128)(2,1)S(1)}, u32[]{:S(2)}, u32[]{:S(2)}) collective-permute-start(bf16[128,1024]{1,0:T(8,128)(2,1)S(1)} %get-tuple-element.169), channel_id=1, source_target_pairs={{0,4},{1,5},{2,6},{3,7},{4,0},{5,1},{6,2},{7,3},{8,12},{9,13},{10,... | collective-permute-start | bytes 786440 | tf_op jit(solution)/shard_map/ppermute | solution.py:87
  153.6 11.2 %collective-permute-start.34 = (bf16[128,1024]{1,0:T(8,128)(2,1)S(1)}, bf16[128,1024]{1,0:T(8,128)(2,1)S(1)}, u32[]{:S(2)}, u32[]{:S(2)}) collective-permute-start(bf16[128,1024]{1,0:T(8,128)(2,1)S(1)} %get-tuple-element.170), channel_id=1, source_target_pairs={{0,8},{1,9},{2,10},{3,11},{4,12},{5,13},{6,14},{7,15},{8,0},{9,1},... | collective-permute-start | bytes 786440 | tf_op jit(solution)/shard_map/ppermute | solution.py:87
  154.3 18.4 %collective-permute-start.35 = (bf16[128,1024]{1,0:T(8,128)(2,1)S(1)}, bf16[128,1024]{1,0:T(8,128)(2,1)S(1)}, u32[]{:S(2)}, u32[]{:S(2)}) collective-permute-start(bf16[128,1024]{1,0:T(8,128)(2,1)S(1)} %get-tuple-element.171), channel_id=1, source_target_pairs={{0,12},{1,13},{2,14},{3,15},{4,8},{5,9},{6,10},{7,11},{8,4},{9,5},... | collective-permute-start | bytes 786440 | tf_op jit(solution)/shard_map/ppermute | solution.py:87
  172.7 8.2 %collective-permute-start.36 = (bf16[12400,128]{1,0:T(8,128)(2,1)S(1)}, bf16[12400,128]{1,0:T(8,128)(2,1)S(1)}, u32[]{:S(2)}, u32[]{:S(2)}) collective-permute-start(bf16[12400,128]{1,0:T(8,128)(2,1)S(1)} %get-tuple-element.180), channel_id=1, source_target_pairs={{0,16},{1,17},{2,18},{3,19},{4,20},{5,21},{6,22},{7,23},{8,24},{9,... | collective-permute-start | bytes 9523208 | tf_op jit(solution)/shard_map/ppermute | solution.py:87
  180.9 22.8 %copy-start.15 = (bf16[2,128,1024]{2,1,0:T(8,128)(2,1)S(1)}, bf16[2,128,1024]{2,1,0:T(8,128)(2,1)}, u32[]{:S(2)}) copy-start(bf16[2,128,1024]{2,1,0:T(8,128)(2,1)} %get-tuple-element.208) | copy-start | bytes 1572868
  181.7 23.7 %collective-permute-start.37 = (bf16[6256,128]{1,0:T(8,128)(2,1)S(1)}, bf16[6256,128]{1,0:T(8,128)(2,1)S(1)}, u32[]{:S(2)}, u32[]{:S(2)}) collective-permute-start(bf16[6256,128]{1,0:T(8,128)(2,1)S(1)} %get-tuple-element.183), channel_id=1, source_target_pairs={{0,2},{1,3},{2,0},{3,1},{4,6},{5,7},{6,4},{7,5},{8,10},{9,11},{10,... | collective-permute-start | bytes 4804616 | tf_op jit(solution)/shard_map/ppermute | solution.py:87
  181.9 16.1 %collective-permute-start.39 = (bf16[128,1024]{1,0:T(8,128)(2,1)S(1)}, bf16[128,1024]{1,0:T(8,128)(2,1)S(1)}, u32[]{:S(2)}, u32[]{:S(2)}) collective-permute-start(bf16[128,1024]{1,0:T(8,128)(2,1)S(1)} %fusion.18.refs_0_), channel_id=1, source_target_pairs={{0,8},{1,9},{2,10},{3,11},{4,12},{5,13},{6,14},{7,15},{8,0},{9,1},... | collective-permute-start | bytes 786440 | tf_op jit(solution)/shard_map/ppermute | solution.py:87
  187.3 10.7 %collective-permute-start.38 = (bf16[128,1024]{1,0:T(8,128)(2,1)S(1)}, bf16[128,1024]{1,0:T(8,128)(2,1)S(1)}, u32[]{:S(2)}, u32[]{:S(2)}) collective-permute-start(bf16[128,1024]{1,0:T(8,128)(2,1)S(1)} %fusion.18.refs_0_), channel_id=1, source_target_pairs={{0,4},{1,5},{2,6},{3,7},{4,0},{5,1},{6,2},{7,3},{8,12},{9,13},{10,... | collective-permute-start | bytes 786440 | tf_op jit(solution)/shard_map/ppermute | solution.py:87
  198.0 5.6 %collective-permute-start.40 = (bf16[128,1024]{1,0:T(8,128)(2,1)S(1)}, bf16[128,1024]{1,0:T(8,128)(2,1)S(1)}, u32[]{:S(2)}, u32[]{:S(2)}) collective-permute-start(bf16[128,1024]{1,0:T(8,128)(2,1)S(1)} %collective-permute-done.39.refs_2_), channel_id=1, source_target_pairs={{0,4},{1,5},{2,6},{3,7},{4,0},{5,1},{6,2},{7,3},{8,12},{9,13},{10,... | collective-permute-start | bytes 786440 | tf_op jit(solution)/shard_map/ppermute | solution.py:87
  203.6 17.2 %collective-permute-start.46 = (bf16[2,128,1024]{2,1,0:T(8,128)(2,1)S(1)}, bf16[2,128,1024]{2,1,0:T(8,128)(2,1)S(1)}, u32[]{:S(2)}, u32[]{:S(2)}) collective-permute-start(bf16[2,128,1024]{2,1,0:T(8,128)(2,1)S(1)} %copy-done.15), channel_id=1, source_target_pairs={{0,4},{1,5},{2,6},{3,7},{4,0},{5,1},{6,2},{7,3},{8,12},{9,13},{10,... | collective-permute-start | bytes 1572872 | tf_op jit(solution)/shard_map/ppermute | solution.py:87
  205.8 15.1 %collective-permute-start.41 = (bf16[3184,128]{1,0:T(8,128)(2,1)S(1)}, bf16[3184,128]{1,0:T(8,128)(2,1)S(1)}, u32[]{:S(2)}, u32[]{:S(2)}) collective-permute-start(bf16[3184,128]{1,0:T(8,128)(2,1)S(1)} %get-tuple-element.185), channel_id=1, source_target_pairs={{0,1},{1,0},{2,3},{3,2},{4,5},{5,4},{6,7},{7,6},{8,9},{9,8},{10,11... | collective-permute-start | bytes 2445320 | tf_op jit(solution)/shard_map/ppermute | solution.py:87
  221.2 6.8 %collective-permute-start.47 = (bf16[12400,128]{1,0:T(8,128)(2,1)S(1)}, bf16[12400,128]{1,0:T(8,128)(2,1)S(1)}, u32[]{:S(2)}, u32[]{:S(2)}) collective-permute-start(bf16[12400,128]{1,0:T(8,128)(2,1)S(1)} %get-tuple-element.210), channel_id=1, source_target_pairs={{0,16},{1,17},{2,18},{3,19},{4,20},{5,21},{6,22},{7,23},{8,24},{9,... | collective-permute-start | bytes 9523208 | tf_op jit(solution)/shard_map/ppermute | solution.py:87
  228.6 19.9 %collective-permute-start.48 = (bf16[6256,128]{1,0:T(8,128)(2,1)S(1)}, bf16[6256,128]{1,0:T(8,128)(2,1)S(1)}, u32[]{:S(2)}, u32[]{:S(2)}) collective-permute-start(bf16[6256,128]{1,0:T(8,128)(2,1)S(1)} %get-tuple-element.212), channel_id=1, source_target_pairs={{0,2},{1,3},{2,0},{3,1},{4,6},{5,7},{6,4},{7,5},{8,10},{9,11},{10,... | collective-permute-start | bytes 4804616 | tf_op jit(solution)/shard_map/ppermute | solution.py:87
  230.0 18.9 %collective-permute-start.49 = (bf16[128,1024]{1,0:T(8,128)(2,1)S(1)}, bf16[128,1024]{1,0:T(8,128)(2,1)S(1)}, u32[]{:S(2)}, u32[]{:S(2)}) collective-permute-start(bf16[128,1024]{1,0:T(8,128)(2,1)S(1)} %fusion.29), channel_id=1, source_target_pairs={{0,8},{1,9},{2,10},{3,11},{4,12},{5,13},{6,14},{7,15},{8,0},{9,1},... | collective-permute-start | bytes 786440 | tf_op jit(solution)/shard_map/ppermute | solution.py:87
  231.1 17.9 %collective-permute-start.42 = (bf16[560,128]{1,0:T(8,128)(2,1)S(1)}, bf16[560,128]{1,0:T(8,128)(2,1)S(1)}, u32[]{:S(2)}, u32[]{:S(2)}) collective-permute-start(bf16[560,128]{1,0:T(8,128)(2,1)S(1)} %get-tuple-element.201), channel_id=1, source_target_pairs={{0,4},{1,5},{2,6},{3,7},{4,0},{5,1},{6,2},{7,3},{8,12},{9,13},{10,... | collective-permute-start | bytes 430088 | tf_op jit(solution)/shard_map/ppermute | solution.py:87
  231.5 17.4 %collective-permute-start.43 = (bf16[560,128]{1,0:T(8,128)(2,1)S(1)}, bf16[560,128]{1,0:T(8,128)(2,1)S(1)}, u32[]{:S(2)}, u32[]{:S(2)}) collective-permute-start(bf16[560,128]{1,0:T(8,128)(2,1)S(1)} %get-tuple-element.202), channel_id=1, source_target_pairs={{0,8},{1,9},{2,10},{3,11},{4,12},{5,13},{6,14},{7,15},{8,0},{9,1},... | collective-permute-start | bytes 430088 | tf_op jit(solution)/shard_map/ppermute | solution.py:87
  233.4 15.5 %collective-permute-start.44 = (bf16[560,128]{1,0:T(8,128)(2,1)S(1)}, bf16[560,128]{1,0:T(8,128)(2,1)S(1)}, u32[]{:S(2)}, u32[]{:S(2)}) collective-permute-start(bf16[560,128]{1,0:T(8,128)(2,1)S(1)} %get-tuple-element.203), channel_id=1, source_target_pairs={{0,12},{1,13},{2,14},{3,15},{4,8},{5,9},{6,10},{7,11},{8,4},{9,5},... | collective-permute-start | bytes 430088 | tf_op jit(solution)/shard_map/ppermute | solution.py:87
  249.0 16.6 %collective-permute-start.50 = (bf16[3184,128]{1,0:T(8,128)(2,1)S(1)}, bf16[3184,128]{1,0:T(8,128)(2,1)S(1)}, u32[]{:S(2)}, u32[]{:S(2)}) collective-permute-start(bf16[3184,128]{1,0:T(8,128)(2,1)S(1)} %get-tuple-element.216), channel_id=1, source_target_pairs={{0,1},{1,0},{2,3},{3,2},{4,5},{5,4},{6,7},{7,6},{8,9},{9,8},{10,11... | collective-permute-start | bytes 2445320 | tf_op jit(solution)/shard_map/ppermute | solution.py:87
  251.0 14.6 %collective-permute-start.45 = (bf16[2,128,1024]{2,1,0:T(8,128)(2,1)S(1)}, bf16[2,128,1024]{2,1,0:T(8,128)(2,1)S(1)}, u32[]{:S(2)}, u32[]{:S(2)}) collective-permute-start(bf16[2,128,1024]{2,1,0:T(8,128)(2,1)S(1)} %get-tuple-element.204), channel_id=1, source_target_pairs={{0,4},{1,5},{2,6},{3,7},{4,0},{5,1},{6,2},{7,3},{8,12},{9,13},{10,... | collective-permute-start | bytes 1572872 | tf_op jit(solution)/shard_map/ppermute | solution.py:87
  266.6 7.7 %collective-permute-start.51 = (bf16[560,128]{1,0:T(8,128)(2,1)S(1)}, bf16[560,128]{1,0:T(8,128)(2,1)S(1)}, u32[]{:S(2)}, u32[]{:S(2)}) collective-permute-start(bf16[560,128]{1,0:T(8,128)(2,1)S(1)} %get-tuple-element.219), channel_id=1, source_target_pairs={{0,4},{1,5},{2,6},{3,7},{4,0},{5,1},{6,2},{7,3},{8,12},{9,13},{10,... | collective-permute-start | bytes 430088 | tf_op jit(solution)/shard_map/ppermute | solution.py:87
  266.6 7.7 %collective-permute-start.52 = (bf16[560,128]{1,0:T(8,128)(2,1)S(1)}, bf16[560,128]{1,0:T(8,128)(2,1)S(1)}, u32[]{:S(2)}, u32[]{:S(2)}) collective-permute-start(bf16[560,128]{1,0:T(8,128)(2,1)S(1)} %get-tuple-element.220), channel_id=1, source_target_pairs={{0,8},{1,9},{2,10},{3,11},{4,12},{5,13},{6,14},{7,15},{8,0},{9,1},... | collective-permute-start | bytes 430088 | tf_op jit(solution)/shard_map/ppermute | solution.py:87
  268.2 8.8 %collective-permute-start.53 = (bf16[560,128]{1,0:T(8,128)(2,1)S(1)}, bf16[560,128]{1,0:T(8,128)(2,1)S(1)}, u32[]{:S(2)}, u32[]{:S(2)}) collective-permute-start(bf16[560,128]{1,0:T(8,128)(2,1)S(1)} %get-tuple-element.221), channel_id=1, source_target_pairs={{0,12},{1,13},{2,14},{3,15},{4,8},{5,9},{6,10},{7,11},{8,4},{9,5},... | collective-permute-start | bytes 430088 | tf_op jit(solution)/shard_map/ppermute | solution.py:87
  277.7 5.2 %collective-permute-start.55 = (f32[8,128]{1,0:T(8,128)S(1)}, f32[8,128]{1,0:T(8,128)S(1)}, u32[]{:S(2)}, u32[]{:S(2)}) collective-permute-start(f32[8,128]{1,0:T(8,128)S(1)} %get-tuple-element.226), channel_id=1, source_target_pairs={{0,16},{1,17},{2,18},{3,19},{4,20},{5,21},{6,22},{7,23},{8,24},{9,... | collective-permute-start | bytes 12296 | tf_op jit(solution)/shard_map/ppermute | solution.py:87
  282.1 8.6 %collective-permute-start.58 = (bf16[3072,128]{1,0:T(8,128)(2,1)S(1)}, bf16[3072,128]{1,0:T(8,128)(2,1)S(1)}, u32[]{:S(2)}, u32[]{:S(2)}) collective-permute-start(bf16[3072,128]{1,0:T(8,128)(2,1)S(1)} %get-tuple-element.227), channel_id=1, source_target_pairs={{0,16},{1,17},{2,18},{3,19},{4,20},{5,21},{6,22},{7,23},{8,24},{9,... | collective-permute-start | bytes 2359304 | tf_op jit(solution)/shard_map/ppermute | solution.py:87
  282.9 2.5 collective-permute-start.56
  283.1 7.6 %collective-permute-start.54 = (bf16[128,1024]{1,0:T(8,128)(2,1)S(1)}, bf16[128,1024]{1,0:T(8,128)(2,1)S(1)}, u32[]{:S(2)}, u32[]{:S(2)}) collective-permute-start(bf16[128,1024]{1,0:T(8,128)(2,1)S(1)} %fusion.28), channel_id=1, source_target_pairs={{0,8},{1,9},{2,10},{3,11},{4,12},{5,13},{6,14},{7,15},{8,0},{9,1},... | collective-permute-start | bytes 786440 | tf_op jit(solution)/shard_map/ppermute | solution.py:87
  285.4 2.5 collective-permute-start.57
  293.0 14.6 %collective-permute-start.59 = (bf16[2,128,1024]{2,1,0:T(8,128)(2,1)}, bf16[2,128,1024]{2,1,0:T(8,128)(2,1)}, u32[]{:S(2)}, u32[]{:S(2)}) collective-permute-start(bf16[2,128,1024]{2,1,0:T(8,128)(2,1)} %broadcast_select_fusion.4), channel_id=1, source_target_pairs={{0,16},{1,17},{2,18},{3,19},{4,20},{5,21},{6,22},{7,23},{8,24},{9,... | collective-permute-start | bytes 1572872 | tf_op jit(solution)/shard_map/ppermute | solution.py:87
  (13 other events, 82.6 us)
